TPU v7x, 256 devices: a whole 4x4x8 slice. The times are simulated.
256 devices in a mesh: ens: 8 (over z), space: 32 (over y, x, core).
Axes of the slice: x: 4, y: 4, z: 8, core: 2. Of those that a mesh axis runs over, the one named last changes fastest.
Arguments:
- mesh_latent: bfloat16 [8, 2048, 1024], P('ens', 'space'), may hold values from -6 to 6
- grid_latent: bfloat16 [8192, 1024], P('space'), may hold values from -6 to 6
- edge_list: int32 [8192, 3], P('space'), may hold values from 0 to 2047, as said below
- target: float32 [8192, 100], P('space'), may hold values from -6 to 6
- cell_area: float32 [8192], P('space'), may hold values from 0.3 to 3
- var_weight: float32 [100], replicated, may hold values from 0.1 to 1
- w_query: bfloat16 [1024, 1024], replicated, may hold values from -0.1875 to 0.1875
- w_key: bfloat16 [1024, 1024], replicated, may hold values from -0.1875 to 0.1875
- w_value: bfloat16 [1024, 1024], replicated, may hold values from -0.1875 to 0.1875
- w_out_proj: bfloat16 [1024, 1024], replicated, may hold values from -0.1875 to 0.1875
- w_head: bfloat16 [1024, 100], replicated, may hold values from -0.1875 to 0.1875
Outputs:
- grad_query: float32 [1024, 1024], P('space')
- grad_key: float32 [1024, 1024], P('space')
- grad_value: float32 [1024, 1024], P('space')
- grad_proj: float32 [1024, 1024], P('space')
- grad_head: float32 [1024, 100], P('space')
Inputs may be any that keep to these rules, and one draw needn't show every extreme that they name: `edge_list`: grid point g refers only to mesh nodes held by spatial block g // 256 or the blocks just before and after it, counted cyclically over the 32 blocks.
All inputs are finite; a program needn't handle non-finite values.
Results may differ from a plain program's by a relative error of at most 0.03.
Values may be sent and summed in bfloat16 or wider, within the bound.
A program may use at most 128 MiB of HBM per device.

v0:
```python
import jax
import jax.numpy as jnp
from jax import lax
from jax.sharding import PartitionSpec as P

HEADS = 16
KNN = 3


FAIR_ALPHA = 0.95
SMOOTH_SQ = 0.0625


def with_halo(x, sides, width):
    for axis, dim in sides:
        devices, length = (lax.axis_size(axis), x.shape[dim])
        up = [(i, (i + 1) % devices) for i in range(devices)]
        down = [(j, i) for i, j in up]
        last = lax.slice_in_dim(x, length - width, length, axis=dim)
        first = lax.slice_in_dim(x, 0, width, axis=dim)
        before = lax.ppermute(last, axis, up)
        after = lax.ppermute(first, axis, down)
        x = jnp.concatenate([before, x, after], axis=dim)
    return x


def shifted(block, axis, distance):
    devices = range(lax.axis_size(axis))
    route = [((i - distance) % len(devices), i) for i in devices]
    return lax.ppermute(block, axis, route)


def smooth_slope(diff):
    return diff / jnp.sqrt(diff * diff + SMOOTH_SQ)


def forward_local(grid_rows, key_table, value_table, index_rows, w_query, w_out_proj, w_head):
    row_count, model_width = grid_rows.shape
    head_size = model_width // HEADS
    queries = (
        jnp.dot(grid_rows, w_query, preferred_element_type=jnp.float32)
        .astype(jnp.bfloat16)
        .reshape(row_count, HEADS, head_size)
    )
    key_rows = jnp.take(key_table, index_rows, axis=0).reshape(row_count, KNN, HEADS, head_size)
    value_rows = jnp.take(value_table, index_rows, axis=0).reshape(row_count, KNN, HEADS, head_size)
    scores = jnp.einsum(
        "ghd,gkhd->ghk", queries, key_rows, preferred_element_type=jnp.float32
    ) * head_size ** (-0.5)
    attention = jax.nn.softmax(scores, axis=-1)
    attention_low = attention.astype(jnp.bfloat16)
    attended = (
        jnp.einsum("ghk,gkhd->ghd", attention_low, value_rows, preferred_element_type=jnp.float32)
        .astype(jnp.bfloat16)
        .reshape(row_count, model_width)
    )
    hidden = (
        grid_rows.astype(jnp.float32)
        + jnp.dot(attended, w_out_proj, preferred_element_type=jnp.float32)
    ).astype(jnp.bfloat16)
    prediction = jnp.dot(hidden, w_head, preferred_element_type=jnp.float32)
    return (prediction, (queries, key_rows, value_rows, attention, attention_low, attended, hidden))


def backward_local(saved_state, grad_pred, grid_rows, w_out_proj, w_head):
    queries, key_rows, value_rows, attention, attention_low, attended, hidden = saved_state
    row_count, model_width = grid_rows.shape
    head_size = model_width // HEADS
    grad_low = grad_pred.astype(jnp.bfloat16)
    grad_head = jnp.dot(hidden.T, grad_low, preferred_element_type=jnp.float32)
    grad_hidden = jnp.dot(grad_low, w_head.T, preferred_element_type=jnp.float32).astype(
        jnp.bfloat16
    )
    grad_proj = jnp.dot(attended.T, grad_hidden, preferred_element_type=jnp.float32)
    grad_att = (
        jnp.dot(grad_hidden, w_out_proj.T, preferred_element_type=jnp.float32)
        .astype(jnp.bfloat16)
        .reshape(row_count, HEADS, head_size)
    )
    grad_weight = jnp.einsum(
        "ghd,gkhd->ghk", grad_att, value_rows, preferred_element_type=jnp.float32
    )
    grad_values = (
        jnp.einsum("ghk,ghd->gkhd", attention_low, grad_att, preferred_element_type=jnp.float32)
        .astype(jnp.bfloat16)
        .reshape(row_count * KNN, model_width)
    )
    grad_scores = (
        attention
        * (grad_weight - jnp.sum(attention * grad_weight, axis=-1, keepdims=True))
        * head_size ** (-0.5)
    ).astype(jnp.bfloat16)
    grad_queries = (
        jnp.einsum("ghk,gkhd->ghd", grad_scores, key_rows, preferred_element_type=jnp.float32)
        .astype(jnp.bfloat16)
        .reshape(row_count, model_width)
    )
    grad_keys = (
        jnp.einsum("ghk,ghd->gkhd", grad_scores, queries, preferred_element_type=jnp.float32)
        .astype(jnp.bfloat16)
        .reshape(row_count * KNN, model_width)
    )
    grad_query = jnp.dot(grid_rows.T, grad_queries, preferred_element_type=jnp.float32)
    return (grad_query, grad_proj, grad_head, grad_keys, grad_values)


def crps_grad(prediction, pair_sum, target_rows, area_rows, var_weight, members):
    fair_eps = (1.0 - FAIR_ALPHA) / members
    pair_coef = (1.0 - fair_eps) / (members * (members - 1))
    scaled = smooth_slope(prediction - target_rows) / members - pair_coef * pair_sum
    return area_rows[:, None] * var_weight[None, :] * scaled


def local(
    mesh_latent,
    grid_latent,
    edge_list,
    target,
    cell_area,
    var_weight,
    w_query,
    w_key,
    w_value,
    w_out_proj,
    w_head,
):
    latent = mesh_latent[0]
    mesh_rows = latent.shape[0]
    model_width = latent.shape[1]
    shard_count = lax.axis_size("space")
    position = lax.axis_index("space")
    owner_shard = edge_list // mesh_rows
    local_index = (owner_shard - position + 1) % shard_count * mesh_rows + edge_list % mesh_rows
    own_keys = jnp.dot(latent, w_key, preferred_element_type=jnp.float32).astype(jnp.bfloat16)
    own_values = jnp.dot(latent, w_value, preferred_element_type=jnp.float32).astype(jnp.bfloat16)
    stacked = with_halo(jnp.stack([own_keys, own_values]), (("space", 1),), mesh_rows)
    key_table = stacked[0]
    value_table = stacked[1]
    prediction, saved_state = forward_local(
        grid_latent, key_table, value_table, local_index, w_query, w_out_proj, w_head
    )
    members = lax.axis_size("ens")
    ensemble = lax.all_gather(prediction[None], "ens", axis=0, tiled=True)
    pair_sum = jnp.sum(smooth_slope(prediction[None] - ensemble), axis=0)
    grad_pred = crps_grad(prediction, pair_sum, target, cell_area, var_weight, members)
    grad_query, grad_proj, grad_head, grad_keys, grad_values = backward_local(
        saved_state, grad_pred, grid_latent, w_out_proj, w_head
    )
    flat_index = local_index.reshape(-1)
    table_rows = 3 * mesh_rows
    selector = (jnp.arange(table_rows, dtype=jnp.int32)[:, None] == flat_index[None, :]).astype(
        jnp.bfloat16
    )
    both_grads = jnp.concatenate([grad_keys, grad_values], axis=1)
    table_sums = jnp.dot(selector, both_grads, preferred_element_type=jnp.float32)
    from_next = shifted(table_sums[:mesh_rows], "space", -1)
    from_prior = shifted(table_sums[2 * mesh_rows :], "space", 1)
    owned_sums = table_sums[mesh_rows : 2 * mesh_rows] + from_next + from_prior
    owned_high = owned_sums.astype(jnp.bfloat16)
    owned_low = (owned_sums - owned_high.astype(jnp.float32)).astype(jnp.bfloat16)
    grad_both = jnp.dot(latent.T, owned_high, preferred_element_type=jnp.float32) + jnp.dot(
        latent.T, owned_low, preferred_element_type=jnp.float32
    )
    grad_key = grad_both[:, :model_width]
    grad_value = grad_both[:, model_width:]
    reduced = (
        lax.psum_scatter(grad_query, "space", scatter_dimension=0, tiled=True),
        lax.psum_scatter(grad_key, "space", scatter_dimension=0, tiled=True),
        lax.psum_scatter(grad_value, "space", scatter_dimension=0, tiled=True),
        lax.psum_scatter(grad_proj, "space", scatter_dimension=0, tiled=True),
        lax.psum_scatter(grad_head, "space", scatter_dimension=0, tiled=True),
    )
    summed = lax.psum((reduced[0], reduced[1], reduced[2], reduced[3], reduced[4]), "ens")
    return (summed[0], summed[1], summed[2], summed[3], summed[4])


def solution(mesh):
    in_specs = (
        P("ens", "space", None),
        P("space", None),
        P("space", None),
        P("space", None),
        P("space"),
        P(),
        P(),
        P(),
        P(),
        P(),
        P(),
    )
    out_specs = (
        P("space", None),
        P("space", None),
        P("space", None),
        P("space", None),
        P("space", None),
    )
    return jax.shard_map(local, mesh=mesh, in_specs=in_specs, out_specs=out_specs, check_vma=False)
```

profile of v0, /device:TPU:1, one launch (start us, length us, event | category | flops | bytes accessed | tf_op | source)
XLA Modules:
  0.0 660.3 jit_solution(11631935919327218486)
XLA Ops:
  7.3 2.3 fusion.18
  10.2 3.3 collective-permute-start.1
  14.1 3.1 convolution_convert_fusion.1
  20.8 3.6 gather_fusion.1
  24.4 5.1 reshape.82
  29.5 3.6 gather_fusion
  33.1 5.1 reshape.78
  38.2 5.0 broadcast_select_fusion
  43.3 4.1 copy.77
  47.4 4.2 copy.76
  51.6 1.9 multiply_reduce_fusion.3
  54.5 2.8 convert_convert_fusion
  58.5 1.9 multiply_reduce_fusion.2
  61.8 23.3 %all-gather = f32[2048,100]{0,1:T(8,128)S(1)} all-gather(f32[256,100]{0,1:T(8,128)S(1)} %fusion.47), channel_id=2, replica_groups=mesh['ens'=8,'space'=32] {'ens'}, dimensions={0}, use_global_device_ids=true | all-gather | bytes 921600 | tf_op jit(solution)/shard_map/all_gather | solution.py:143
  87.0 1.5 convolution_convert_fusion
  88.5 1.4 copy.43
  92.5 2.0 fusion.17
  95.7 3.7 convolution_bitcast_fusion
  99.4 5.4 copy.80
  105.0 2.6 copy.45
  107.8 2.5 copy.46
  110.2 4.9 fusion.4
  115.1 5.5 reshape.53
  120.6 3.3 fusion.3
  123.9 5.6 reshape.52
  129.5 2.2 fusion.5
  131.8 13.2 %collective-permute-start.2 = (f32[64,2048]{1,0:T(8,128)S(1)}, f32[64,2048]{1,0:T(8,128)S(1)}, u32[]{:S(2)}, u32[]{:S(2)}) collective-permute-start(f32[64,2048]{1,0:T(8,128)S(1)} %get-tuple-element.29), channel_id=1, source_target_pairs={{1,0},{2,1},{3,2},{4,3},{5,4},{6,5},{7,6},{8,7},{9,8},{10,9},{11,1... | collective-permute-start | bytes 1572872 | tf_op jit(solution)/shard_map/ppermute | solution.py:30
  145.0 1.5 collective-permute-done.2
  146.6 4.6 collective-permute-done.3
  152.4 1.3 add_bitcast_fusion
  153.7 4.0 fusion.43
  157.8 5.4 copy.84
  163.2 5.4 copy.82
  169.9 2.6 fusion.48
  174.8 24.7 %reduce-scatter.16.cloned.1.call-done = f32[32,1024]{1,0:T(8,128)} async-done(((f32[1024,1024]{1,0:T(8,128)}), f32[32,1024]{1,0:T(8,128)}) %reduce-scatter.16.cloned.1.call-update) | async-done | bytes 131088
  199.5 1.9 copy.81
  201.4 91.5 %reduce-scatter.20.cloned.1.call-done = f32[32,1024]{1,0:T(8,128)} async-done(((f32[1024,1024]{1,0:T(8,128)}), f32[32,1024]{1,0:T(8,128)}) %reduce-scatter.20.cloned.1.call-update) | async-done | bytes 131088
  292.9 1.9 copy.85
  294.8 91.0 %reduce-scatter.18.cloned.1.call-done = f32[32,1024]{1,0:T(8,128)} async-done(((f32[1024,1024]{1,0:T(8,128)}), f32[32,1024]{1,0:T(8,128)}) %reduce-scatter.18.cloned.1.call-update) | async-done | bytes 131088
  385.8 2.1 copy.83
  387.9 91.2 %reduce-scatter.12.cloned.1.call-done = f32[32,1024]{1,0:T(8,128)} async-done(((f32[1024,1024]{1,0:T(8,128)}), f32[32,1024]{1,0:T(8,128)}) %reduce-scatter.12.cloned.1.call-update) | async-done | bytes 131088 | tf_op jit(solution)/shard_map/reduce_scatter | solution.py:170
  479.1 87.3 %reduce-scatter.14.cloned.1.call-done = f32[32,100]{1,0:T(8,128)} async-done(((f32[1024,100]{1,0:T(8,128)}), f32[32,100]{1,0:T(8,128)}) %reduce-scatter.14.cloned.1.call-update) | async-done | bytes 12816 | tf_op jit(solution)/shard_map/reduce_scatter | solution.py:171
  566.4 25.0 %psum.39 = f32[32,100]{1,0:T(8,128)} all-reduce(f32[32,100]{1,0:T(8,128)} %reduce-scatter.14.cloned.1.call-done), channel_id=1, replica_groups=mesh['ens'=8,'space'=32] {'ens'}, use_global_device_ids=true, to_apply=%region_13.15 | all-reduce | flops 3200 | bytes 25600 | tf_op jit(solution)/shard_map/psum | solution.py:173
  591.4 54.9 %all-reduce.3.cloned.1.call-done = (f32[32,1024]{0,1:T(8,128)}, f32[32,1024]{0,1:T(8,128)}, f32[32,1024]{0,1:T(8,128)}, f32[32,1024]{1,0:T(8,128)}) async-done(((f32[32,1024]{0,1:T(8,128)}, f32[32,1024]{0,1:T(8,128)}, f32[32,1024]{0,1:T(8,128)}, f32[32,1024]{1,0:T(8,128)}), (f32[32,1024]{0,1:T(8,128)}, f32[32,1024]{0,1:T(8,128)}, f32[32,1024]{0,1:T(8,128)}, ...) | async-done | bytes 524304 | tf_op jit(solution)/shard_map/psum | solution.py:173
  646.3 1.9 copy.47
  648.1 1.9 copy.48
  650.0 1.9 copy.49
  651.9 1.6 copy.97
  (100 shorter events, 19.2 us)
Async XLA Ops:
  7.2 53.2 %copy-start = (bf16[1024,1024]{1,0:T(8,128)(2,1)S(1)}, bf16[1024,1024]{1,0:T(8,128)(2,1)}, u32[]{:S(2)}) copy-start(bf16[1024,1024]{1,0:T(8,128)(2,1)} %param.22) | copy-start | bytes 6291460
  7.2 2.4 copy-start.12
  7.2 6.3 copy-start.24
  7.2 192.3 %reduce-scatter.16.cloned.1.call-start = ((), (), s32[]{:S(2)}) async-start(), calls=%async_computation.7 | async-start | bytes 4325376
  7.2 2.4 copy-start.17
  9.7 4.4 copy-start.13
  10.2 9.4 %collective-permute-start.1 = (bf16[2,64,1024]{2,1,0:T(8,128)(2,1)S(1)}, bf16[2,64,1024]{2,1,0:T(8,128)(2,1)}, u32[]{:S(2)}, u32[]{:S(2)}) collective-permute-start(bf16[2,64,1024]{2,1,0:T(8,128)(2,1)S(1)} %pad_maximum_fusion.1), channel_id=1, source_target_pairs={{1,0},{2,1},{3,2},{4,3},{5,4},{6,5},{7,6},{8,7},{9,8},{10,9},{11,1... | collective-permute-start | bytes 786440 | tf_op jit(solution)/shard_map/ppermute | solution.py:22
  13.5 6.1 collective-permute-start
  47.4 4.2 copy-start.4
  58.5 1.9 copy-start.14
  60.4 1.5 copy-start.8
  60.4 1.1 copy-start.22
  61.5 24.2 %copy-start.10 = (bf16[256,1024]{1,0:T(8,128)(2,1)}, bf16[256,1024]{1,0:T(8,128)(2,1)S(1)}, u32[]{:S(2)}) copy-start(bf16[256,1024]{1,0:T(8,128)(2,1)S(1)} %fusion.9) | copy-start | bytes 1572868
  61.5 24.2 %copy-start.23 = (f32[256,100]{0,1:T(8,128)S(1)}, f32[256,100]{0,1:T(8,128)}, u32[]{:S(2)}) copy-start(f32[256,100]{0,1:T(8,128)} %param.16) | copy-start | bytes 307204
  61.5 24.2 %copy-start.25 = (f32[256]{0:T(256)S(1)}, f32[256]{0:T(256)}, u32[]{:S(2)}) copy-start(f32[256]{0:T(256)} %param.17) | copy-start | bytes 3076
  61.5 24.2 %copy-start.26 = (f32[100]{0:T(128)S(1)}, f32[100]{0:T(128)}, u32[]{:S(2)}) copy-start(f32[100]{0:T(128)} %param.18) | copy-start | bytes 1204
  86.1 0.8 copy-start.15
  88.5 2.4 copy-start.3
  90.0 1.0 copy-start.5
  91.5 3.8 copy-start.2
  94.5 0.8 copy-start.19
  104.8 3.0 copy-start.6
  104.8 188.1 %reduce-scatter.20.cloned.1.call-start = ((), (), s32[]{:S(2)}) async-start(), calls=%async_computation.9 | async-start | bytes 4325376
  107.6 2.7 copy-start.18
  115.1 5.6 copy-start.7
  115.1 5.6 copy-start.20
  123.9 5.6 copy-start.21
  131.8 14.7 %collective-permute-start.2 = (f32[64,2048]{1,0:T(8,128)S(1)}, f32[64,2048]{1,0:T(8,128)S(1)}, u32[]{:S(2)}, u32[]{:S(2)}) collective-permute-start(f32[64,2048]{1,0:T(8,128)S(1)} %get-tuple-element.29), channel_id=1, source_target_pairs={{1,0},{2,1},{3,2},{4,3},{5,4},{6,5},{7,6},{8,7},{9,8},{10,9},{11,1... | collective-permute-start | bytes 1572872 | tf_op jit(solution)/shard_map/ppermute | solution.py:30
  145.0 6.1 collective-permute-start.3
  163.1 222.7 %reduce-scatter.18.cloned.1.call-start = ((), (), s32[]{:S(2)}) async-start(), calls=%async_computation.8 | async-start | bytes 4325376
  168.6 1.1 copy-start.9
  168.6 1.2 copy-start.16
  168.7 310.4 %reduce-scatter.12.cloned.1.call-start = ((), (), s32[]{:S(2)}) async-start(), calls=%async_computation.5 | async-start | bytes 4325376 | tf_op jit(solution)/shard_map/reduce_scatter | solution.py:170
  172.5 1.1 copy-start.11
  172.5 393.9 %reduce-scatter.14.cloned.1.call-start = ((), (), s32[]{:S(2)}) async-start(), calls=%async_computation.6 | async-start | bytes 540672 | tf_op jit(solution)/shard_map/reduce_scatter | solution.py:171
  174.7 471.5 %all-reduce.3.cloned.1.call-start = ((), (), s32[]{:S(2)}) async-start(), calls=%async_computation.10 | async-start | bytes 3407872 | tf_op jit(solution)/shard_map/psum | solution.py:173
  385.8 267.6 %copy-start.1 = (bf16[1024,1024]{1,0:T(8,128)(2,1)S(1)}, bf16[1024,1024]{1,0:T(8,128)(2,1)}, u32[]{:S(2)}) copy-start(bf16[1024,1024]{1,0:T(8,128)(2,1)} %param.22) | copy-start | bytes 6291460
Sparse Core Ops, SparseCore 0:
  104.9 94.5 reduce-scatter.15
  204.0 88.8 reduce-scatter.19
  296.8 88.9 reduce-scatter.17
  390.1 88.9 reduce-scatter.11
  482.7 83.7 reduce-scatter.13
  568.9 77.2 all-reduce.2
where the time goes:
time: 665 us; the launch traced here: 660 us
  waiting for transfers between devices  447 us (67%)
  local copies, waits for them, and re-layouts  87.5 us (13%)
  blocking collectives  48.2 us (7%)
  other arithmetic  25.4 us (4%)
  matrix products  21.1 us (3%)
  starting transfers between devices  16.8 us (3%)
  between operations  14.5 us (2%)
    unnamed x9, waiting for transfers between devices  207 us
    reduce_scatter x1, waiting for transfers between devices, local(): lax.psum_scatter(grad_proj, 'space', scatter_dimension=0, tiled=True)  91.2 us
    reduce_scatter x1, waiting for transfers between devices, local(): lax.psum_scatter(grad_head, 'space', scatter_dimension=0, tiled=True)  87.3 us
    psum x1, waiting for transfers between devices, local(): lax.psum((reduced[0], reduced[1], reduced[2], reduced[3], reduced[4]), 'e...  54.9 us
    unnamed x69, local copies, waits for them, and re-layouts  44.3 us
    psum x1, blocking collectives, local(): lax.psum((reduced[0], reduced[1], reduced[2], reduced[3], reduced[4]), 'e...  25 us
    all_gather x1, blocking collectives, local(): ensemble = lax.all_gather(prediction[None], 'ens', axis=0, tiled=True)  23.3 us
  transfers between devices with their start and end apart: 10, of which 8 were waited for; matrix products, arithmetic and copies ran while one was open for 9% of the time, Pallas kernels for 0%

commit v1 on v0

v1 whole, which is shorter than its diff:
```python
import functools

import jax
import jax.numpy as jnp
from jax import lax
from jax.experimental import pallas as pl
from jax.experimental.pallas import tpu as pltpu
from jax.sharding import PartitionSpec as P

MESH = pl.DeviceIdType.MESH
HEADS = 16
KNN = 3
FAIR_ALPHA = 0.95
SMOOTH_SQ = 0.0625
ENS = 8
SPACE = 32
D = 1024
HD = D // HEADS
G = 256
M = 64
N = 3 * M
E = KNN * G
VAR = 100
VP = 128
C = D // ENS
ROWS = D // SPACE
W = 256
BF = jnp.bfloat16
F32 = jnp.float32


def dot(a, b):
    return jnp.dot(a, b, preferred_element_type=F32)


def slope(d):
    return d * lax.rsqrt(d * d + SMOOTH_SQ)


def same_head(width, value):
    rows = lax.broadcasted_iota(jnp.int32, (width, width), 0) // HD
    cols = lax.broadcasted_iota(jnp.int32, (width, width), 1) // HD
    return jnp.where(rows == cols, value, 0.0).astype(BF)


def softmax3(scores):
    s0, s1, s2 = scores[:G], scores[G : 2 * G], scores[2 * G :]
    top = jnp.maximum(jnp.maximum(s0, s1), s2)
    e0, e1, e2 = jnp.exp(s0 - top), jnp.exp(s1 - top), jnp.exp(s2 - top)
    inv = 1.0 / (e0 + e1 + e2)
    return e0 * inv, e1 * inv, e2 * inv


def main_kernel(
    x_ref, grid_ref, edge_ref, target_ref, area_ref, var_ref,
    wq_hbm, wk_hbm, wv_hbm, wo_hbm, wh_ref,
    out_ref,
    wq, wk, wv, wo, whp, lat, lat_t, grid_t, mix_t, q, keys, values, attended, hidden,
    delta, kvc, wkvc, kgv, att_all, gl, s_all, oh, oh_t, q3s, gq, uct, common, areaw,
    part_ab, part, r_ab, r, rz,
    wsem, ring_s, ring_r, halo_s, halo_l, halo_r, d_s, d_r, ab_s, ab_r, g_s, g_r, z_s, z_r,
):
    e = lax.axis_index("ens")
    s = lax.axis_index("space")

    loads = [
        pltpu.make_async_copy(src, dst, wsem.at[i])
        for i, (src, dst) in enumerate(((wq_hbm, wq), (wk_hbm, wk), (wv_hbm, wv), (wo_hbm, wo)))
    ]
    for load in loads:
        load.start()

    def ens_peer(d):
        return (lax.rem(e + d, ENS), s)

    def space_peer(d):
        return (e, lax.rem(s + d, SPACE))

    barrier = pltpu.get_barrier_semaphore()

    @pl.loop(1, ENS)
    def _(d):
        pl.semaphore_signal(barrier, inc=1, device_id=ens_peer(d), device_id_type=MESH)

    @pl.loop(1, SPACE)
    def _(d):
        pl.semaphore_signal(barrier, inc=1, device_id=space_peer(d), device_id_type=MESH)

    def own_rows(m):
        return pl.ds(pl.multiple_of(m * N + M, M), M)

    def low_rows(m):
        return pl.ds(pl.multiple_of(m * N, M), M)

    def high_rows(m):
        return pl.ds(pl.multiple_of(m * N + 2 * M, M), M)

    def member(d):
        return lax.rem(e + d + ENS, ENS)

    def ring_copy(m, step, way):
        return pltpu.make_async_remote_copy(
            src_ref=lat.at[own_rows(m)], dst_ref=lat.at[own_rows(m)],
            send_sem=ring_s.at[step], recv_sem=ring_r.at[m],
            device_id=ens_peer(way), device_id_type=MESH,
        )

    def halo_copies(m):
        up = pltpu.make_async_remote_copy(
            src_ref=lat.at[own_rows(m)], dst_ref=lat.at[low_rows(m)],
            send_sem=halo_s.at[m, 0], recv_sem=halo_l.at[m],
            device_id=space_peer(1), device_id_type=MESH,
        )
        down = pltpu.make_async_remote_copy(
            src_ref=lat.at[own_rows(m)], dst_ref=lat.at[high_rows(m)],
            send_sem=halo_s.at[m, 1], recv_sem=halo_r.at[m],
            device_id=space_peer(SPACE - 1), device_id_type=MESH,
        )
        return up, down

    def start_halo(m):
        up, down = halo_copies(m)
        up.start()
        down.start()

    lat[own_rows(e), :] = x_ref[...]
    whp[...] = jnp.zeros_like(whp)
    whp[:, :VAR] = wh_ref[...]
    loads[0].wait()

    @pl.loop(0, D // W)
    def _(n):
        cols = pl.ds(pl.multiple_of(n * W, W), W)
        q[:, cols] = dot(grid_ref[...], wq[:, cols]).astype(BF)

    pl.semaphore_wait(barrier, ENS - 1 + SPACE - 1)
    start_halo(e)
    forward = [ring_copy(member(-k + 1), k - 1, 1) for k in range(1, 5)]
    backward = [ring_copy(member(k - 1), 3 + k, ENS - 1) for k in range(1, 4)]
    forward[0].start()
    backward[0].start()

    def ring_arrived(m):
        ring_copy(m, 0, 1).wait_recv()
        start_halo(m)

    edges = edge_ref[...]
    slot_rows = (((edges // M) - s + 1 + SPACE) % SPACE) * M + edges % M
    node = lax.broadcasted_iota(jnp.int32, (G, N), 1)
    for j in range(KNN):
        oh[j * G : (j + 1) * G, :] = jnp.where(slot_rows[:, j : j + 1] == node, 1.0, 0.0).astype(BF)
    oh_t[...] = oh[...].T
    grid_t[...] = grid_ref[...].T
    var_row = jnp.concatenate([var_ref[...], jnp.zeros((1, VP - VAR), F32)], axis=1)
    areaw[...] = jnp.broadcast_to(area_ref[...], (VP, G)).T * var_row
    common[...] = dot(grid_ref[...], whp[...])
    loads[1].wait()
    loads[2].wait()
    loads[3].wait()
    hs = pl.ds(pl.multiple_of(e * C, C), C)
    wkvc[:, :C] = wk[:, hs]
    wkvc[:, C:] = wv[:, hs]
    uct[...] = dot(wo[hs, :], whp[...]).T.astype(BF)
    for j in range(KNN):
        q3s[j * G : (j + 1) * G, :] = q[:, hs]

    own_up, own_down = halo_copies(e)
    own_up.wait_recv()
    own_down.wait_recv()
    own_table = pl.ds(pl.multiple_of(e * N, M), N)

    @pl.loop(0, D // W)
    def _(n):
        cols = pl.ds(pl.multiple_of(n * W, W), W)
        keys[:, cols] = dot(lat[own_table, :], wk[:, cols]).astype(BF)
        values[:, cols] = dot(lat[own_table, :], wv[:, cols]).astype(BF)

    ring_arrived(member(-1))
    ring_arrived(member(1))
    forward[1].start()
    backward[1].start()

    @pl.loop(0, D // W)
    def _(n):
        cols = pl.ds(pl.multiple_of(n * W, W), W)
        key_rows = dot(oh[...], keys[:, cols]).astype(BF)
        qc = q[:, cols]
        prod = key_rows * jnp.concatenate([qc, qc, qc], axis=0)
        att = softmax3(dot(prod, same_head(W, HD**-0.5)))
        value_rows = dot(oh[...], values[:, cols])
        total = jnp.zeros((G, W), F32)
        for j in range(KNN):
            total += att[j].astype(BF).astype(F32) * value_rows[j * G : (j + 1) * G]
        attended[:, cols] = total.astype(BF)

    ring_arrived(member(-2))
    ring_arrived(member(2))
    forward[2].start()
    backward[2].start()

    @pl.loop(0, D // W)
    def _(n):
        cols = pl.ds(pl.multiple_of(n * W, W), W)
        update = dot(attended[...], wo[:, cols])
        hidden[:, cols] = (grid_ref[:, cols].astype(F32) + update).astype(BF)

    ring_arrived(member(-3))
    ring_arrived(member(3))
    forward[3].start()

    delta[e] = (dot(hidden[...], whp[...]) - common[...]).astype(BF)

    def delta_copy(d, m):
        return pltpu.make_async_remote_copy(
            src_ref=delta.at[e], dst_ref=delta.at[m],
            send_sem=d_s.at[d], recv_sem=d_r.at[m],
            device_id=ens_peer(d), device_id_type=MESH,
        )

    @pl.loop(1, ENS)
    def _(d):
        delta_copy(d, e).start()

    common[:, :VAR] = common[:, :VAR] - target_ref[...]
    mix_t[:D, :] = attended[...].T
    mix_t[D:, :] = hidden[...].T
    ring_arrived(member(-4))

    def halo_wait(m):
        up, down = halo_copies(m)
        up.wait_recv()
        down.wait_recv()

    @pl.loop(1, ENS)
    def _(d):
        halo_wait(lax.rem(e + d, ENS))

    @pl.loop(0, ENS)
    def _(m):
        table = pl.ds(pl.multiple_of(m * N, M), N)
        kvc[table, :] = dot(lat[table, :], wkvc[...]).astype(BF)
        rows = dot(oh[...], kvc[table, :]).astype(BF)
        kgv[m] = rows
        att = softmax3(dot(rows[:, :C] * q3s[...], same_head(C, HD**-0.5)))
        for j in range(KNN):
            att_all[m, j * G : (j + 1) * G, :] = att[j]

    @pl.loop(0, ENS // 2)
    def _(p):
        both = pl.ds(pl.multiple_of(p * 2 * N, 2 * N), 2 * N)
        lat_t[:, both] = lat[both, :].T

    @pl.loop(1, ENS)
    def _(d):
        delta_copy(d, lax.rem(e + d, ENS)).wait_recv()

    fair_eps = (1.0 - FAIR_ALPHA) / ENS
    pair_coef = (1.0 - fair_eps) / (ENS * (ENS - 1))
    step_rows = 16

    @pl.loop(0, G // step_rows)
    def _(i):
        rows = pl.ds(pl.multiple_of(i * step_rows, step_rows), step_rows)
        dev = [delta[m, rows, :].astype(F32) for m in range(ENS)]
        pair = [None] * ENS
        for a in range(ENS):
            for b in range(a + 1, ENS):
                t = slope(dev[a] - dev[b])
                pair[a] = t if pair[a] is None else pair[a] + t
                pair[b] = -t if pair[b] is None else pair[b] - t
        shift = common[rows, :]
        scale = areaw[rows, :]
        for m in range(ENS):
            grad = scale * (slope(dev[m] + shift) * (1.0 / ENS) - pair_coef * pair[m])
            gl[pl.ds(pl.multiple_of(m * G + i * step_rows, step_rows), step_rows), :] = grad.astype(BF)

    def reduce_copy(src, dst, sends, recvs, d):
        rows = pl.ds(pl.multiple_of(lax.rem(s + d, SPACE) * ROWS, ROWS), ROWS)
        return pltpu.make_async_remote_copy(
            src_ref=src.at[rows], dst_ref=dst.at[d], send_sem=sends.at[d], recv_sem=recvs.at[d],
            device_id=space_peer(d), device_id_type=MESH,
        )

    own_gl = pl.ds(pl.multiple_of(e * G, G), G)

    @pl.loop(0, 2 * D // W)
    def _(i):
        rows = pl.ds(pl.multiple_of(i * W, W), W)
        part = dot(mix_t[rows, :], gl[own_gl, :]).astype(BF)
        target_rows = pl.ds(pl.multiple_of(lax.rem(i, D // W) * W, W), W)
        target_cols = pl.ds(pl.multiple_of((i // (D // W)) * VP, VP), VP)
        part_ab[target_rows, target_cols] = part

    @pl.loop(1, SPACE)
    def _(d):
        reduce_copy(part_ab, r_ab, ab_s, ab_r, d).start()

    gq[...] = jnp.zeros_like(gq)

    @pl.loop(0, ENS)
    def _(m):
        gl_rows = pl.ds(pl.multiple_of(m * G, G), G)
        ga = dot(gl[gl_rows, :], uct[...]).astype(BF)
        ga3 = jnp.concatenate([ga, ga, ga], axis=0)
        gw = dot(kgv[m, :, C:] * ga3, same_head(C, 1.0))
        att = att_all[m]
        t = att * gw
        tot = t[:G] + t[G : 2 * G] + t[2 * G :]
        gs = att * (gw - jnp.concatenate([tot, tot, tot], axis=0)) * HD**-0.5
        gs_low = gs.astype(BF)
        gqe = gs_low.astype(F32) * kgv[m, :, :C].astype(F32)
        gq[...] += gqe[:G] + gqe[G : 2 * G] + gqe[2 * G :]
        edge_grads = jnp.concatenate([gs_low * q3s[...], att.astype(BF) * ga3], axis=1)
        table = pl.ds(pl.multiple_of(m * N, M), N)
        s_all[table, :] = dot(oh_t[...], edge_grads).astype(BF)

    part[:, :C] = dot(grid_t[...], gq[...].astype(BF)).astype(BF)

    @pl.loop(0, D // W)
    def _(i):
        rows = pl.ds(pl.multiple_of(i * W, W), W)
        part[rows, C:] = dot(lat_t[rows, :], s_all[...]).astype(BF)

    @pl.loop(1, SPACE)
    def _(d):
        reduce_copy(part, r, g_s, g_r, d).start()

    own_out = pl.ds(pl.multiple_of(s * ROWS, ROWS), ROWS)
    r_ab[0] = part_ab[own_out, :]
    r[0] = part[own_out, :]

    @pl.loop(1, SPACE)
    def _(d):
        reduce_copy(part_ab, r_ab, ab_s, ab_r, d).wait_recv()

    rz[e, :, 3 * C :] = jnp.sum(r_ab[...].astype(F32), axis=0).astype(BF)

    @pl.loop(1, SPACE)
    def _(d):
        reduce_copy(part, r, g_s, g_r, d).wait_recv()

    rz[e, :, : 3 * C] = jnp.sum(r[...].astype(F32), axis=0).astype(BF)

    def last_copy(d, m):
        return pltpu.make_async_remote_copy(
            src_ref=rz.at[e], dst_ref=rz.at[m], send_sem=z_s.at[d], recv_sem=z_r.at[m],
            device_id=ens_peer(d), device_id_type=MESH,
        )

    @pl.loop(1, ENS)
    def _(d):
        last_copy(d, e).start()

    for copy in forward + backward:
        copy.wait_send()

    @pl.loop(0, ENS)
    def _(m):
        up, down = halo_copies(m)
        up.wait_send()
        down.wait_send()

    @pl.loop(1, ENS)
    def _(d):
        delta_copy(d, e).wait_send()

    @pl.loop(1, SPACE)
    def _(d):
        reduce_copy(part_ab, r_ab, ab_s, ab_r, d).wait_send()
        reduce_copy(part, r, g_s, g_r, d).wait_send()

    @pl.loop(1, ENS)
    def _(d):
        last_copy(d, e).wait_send()
        last_copy(d, lax.rem(e + d, ENS)).wait_recv()

    out_ref[...] = rz[...]


def finish_kernel(rz_ref, wh_ref, q_ref, k_ref, v_ref, p_ref, h_ref):
    for m in range(ENS):
        cols = slice(m * C, (m + 1) * C)
        q_ref[:, cols] = rz_ref[m, :, :C].astype(F32)
        k_ref[:, cols] = rz_ref[m, :, C : 2 * C].astype(F32)
        v_ref[:, cols] = rz_ref[m, :, 2 * C : 3 * C].astype(F32)
    mixed = rz_ref[0, :, 3 * C :].astype(F32)
    for m in range(1, ENS):
        mixed += rz_ref[m, :, 3 * C :].astype(F32)
    h_ref[...] = mixed[:, VP : VP + VAR]
    p_ref[...] = lax.dot_general(
        mixed[:, :VAR].astype(BF), wh_ref[...], (((1,), (1,)), ((), ())), preferred_element_type=F32
    )


def local(x, grid, edges, target, area, var, wq, wk, wv, wo, wh):
    vmem = pl.BlockSpec(memory_space=pltpu.VMEM)
    anywhere = pl.BlockSpec(memory_space=pl.ANY)
    dma = pltpu.SemaphoreType.DMA
    scratch = [
        pltpu.VMEM((D, D), BF), pltpu.VMEM((D, D), BF), pltpu.VMEM((D, D), BF), pltpu.VMEM((D, D), BF),
        pltpu.VMEM((D, VP), BF),
        pltpu.VMEM((ENS * N, D), BF), pltpu.VMEM((D, ENS * N), BF),
        pltpu.VMEM((D, G), BF), pltpu.VMEM((2 * D, G), BF),
        pltpu.VMEM((G, D), BF), pltpu.VMEM((N, D), BF), pltpu.VMEM((N, D), BF),
        pltpu.VMEM((G, D), BF), pltpu.VMEM((G, D), BF),
        pltpu.VMEM((ENS, G, VP), BF),
        pltpu.VMEM((ENS * N, 2 * C), BF), pltpu.VMEM((D, 2 * C), BF),
        pltpu.VMEM((ENS, E, 2 * C), BF), pltpu.VMEM((ENS, E, C), F32),
        pltpu.VMEM((ENS * G, VP), BF), pltpu.VMEM((ENS * N, 2 * C), BF),
        pltpu.VMEM((E, N), BF), pltpu.VMEM((N, E), BF),
        pltpu.VMEM((E, C), BF), pltpu.VMEM((G, C), F32), pltpu.VMEM((VP, C), BF),
        pltpu.VMEM((G, VP), F32), pltpu.VMEM((G, VP), F32),
        pltpu.VMEM((D, 2 * VP), BF), pltpu.VMEM((D, 3 * C), BF),
        pltpu.VMEM((SPACE, ROWS, 2 * VP), BF), pltpu.VMEM((SPACE, ROWS, 3 * C), BF),
        pltpu.VMEM((ENS, ROWS, 3 * C + 2 * VP), BF),
        dma((4,)), dma((7,)), dma((ENS,)), dma((ENS, 2)), dma((ENS,)), dma((ENS,)),
        dma((ENS,)), dma((ENS,)), dma((SPACE,)), dma((SPACE,)), dma((SPACE,)), dma((SPACE,)),
        dma((ENS,)), dma((ENS,)),
    ]
    rz = pl.pallas_call(
        main_kernel,
        out_shape=jax.ShapeDtypeStruct((ENS, ROWS, 3 * C + 2 * VP), BF),
        in_specs=[vmem] * 6 + [anywhere] * 4 + [vmem],
        out_specs=vmem,
        scratch_shapes=scratch,
        compiler_params=pltpu.CompilerParams(
            collective_id=0, has_side_effects=True, vmem_limit_bytes=56 << 20
        ),
        name="ensemble_gradients",
    )(x[0], grid, edges, target, area.reshape(1, G), var.reshape(1, VAR), wq, wk, wv, wo, wh)
    full = jax.ShapeDtypeStruct((ROWS, D), F32)
    return pl.pallas_call(
        finish_kernel,
        out_shape=(full, full, full, full, jax.ShapeDtypeStruct((ROWS, VAR), F32)),
        in_specs=[vmem, vmem],
        out_specs=(vmem,) * 5,
        name="finish",
    )(rz, wh)


def solution(mesh):
    in_specs = (
        P("ens", "space", None),
        P("space", None),
        P("space", None),
        P("space", None),
        P("space"),
        P(),
        P(),
        P(),
        P(),
        P(),
        P(),
    )
    out_specs = (P("space", None),) * 5
    return jax.shard_map(local, mesh=mesh, in_specs=in_specs, out_specs=out_specs, check_vma=False)
```

time: 665 us -> 86.2 us (0.13)
  waiting for transfers between devices: 447 us -> 0 us
  local copies, waits for them, and re-layouts: 87.5 us -> 4.91 us
  Pallas kernels: 0 us -> 80.5 us
  blocking collectives: 48.2 us -> 0 us
  other arithmetic: 25.4 us -> 0 us
  matrix products: 21.1 us -> 0 us
  starting transfers between devices: 16.8 us -> 0 us
  between operations: 14.5 us -> 0.64 us
    unnamed x9 -> x0, waiting for transfers between devices: 207 us -> none
    reduce_scatter x2 -> x0, waiting for transfers between devices: 179 us -> none  [the longest x1 91.2 us: local(): lax.psum_scatter(grad_proj, 'space', scatter_dimension=0, tiled=True)]
    pallas_call x0 -> x2, Pallas kernels: none -> 80.5 us  [the longest x1 78.5 us: local(): pl.pallas_call(main_kernel, out_shape=jax.ShapeDtypeStruct((ENS, ROWS, 3...]
    psum x1 -> x0, waiting for transfers between devices: 54.9 us -> none  [local(): lax.psum((reduced[0], reduced[1], reduced[2], reduced[3], reduced[4]), 'e...]
    unnamed x69 -> x3, local copies, waits for them, and re-layouts: 44.3 us -> 4.91 us
    psum x1 -> x0, blocking collectives: 25 us -> none  [local(): lax.psum((reduced[0], reduced[1], reduced[2], reduced[3], reduced[4]), 'e...]
    all_gather x1 -> x0, blocking collectives: 23.3 us -> none  [local(): ensemble = lax.all_gather(prediction[None], 'ens', axis=0, tiled=True)]
    dot_general x13 -> x0, matrix products: 21.1 us -> none  [the longest x1 3.72 us: backward_local(): jnp.dot(grid_rows.T, grad_queries, preferred_element_type=jnp.float32)]
  transfers between devices with their start and end apart: 10 -> 0, of which waited for: 8 -> 0; matrix products, arithmetic and copies ran while one was open for 9% -> 0% of each run, Pallas kernels for 0% -> 0%
where the time goes in v1:
time: 86.2 us; the launch traced here: 86 us
  Pallas kernels  80.5 us (93%)
  local copies, waits for them, and re-layouts  4.91 us (6%)
    pallas_call x1, Pallas kernels, local(): pl.pallas_call(main_kernel, out_shape=jax.ShapeDtypeStruct((ENS, ROWS, 3...  78.5 us
    unnamed x3, local copies, waits for them, and re-layouts  4.91 us
    pallas_call x1, Pallas kernels, local(): pl.pallas_call(finish_kernel, out_shape=(full, full, full, full, jax.Shap...  1.92 us

profile of v1, /device:TPU:1, one launch (start us, length us, event | category | flops | bytes accessed | tf_op | source)
XLA Modules:
  0.0 86.0 jit_solution(2588072219462987726)
XLA Ops:
  0.6 1.5 %copy.16.edge_ref = s32[256,3]{1,0:T(8,128)} copy(s32[256,3]{0,1:T(4,128)} %param.13) | data formatting | bytes 6144 | tf_op args[2]
  2.1 1.7 %copy.17.target_ref = f32[256,100]{1,0:T(8,128)} copy(f32[256,100]{0,1:T(8,128)} %param.14) | data formatting | bytes 204800 | tf_op args[3]
  3.8 1.8 %copy.18.wh_ref = bf16[1024,100]{1,0:T(8,128)(2,1)} copy(bf16[1024,100]{0,1:T(8,128)(2,1)} %param.21) | data formatting | bytes 409600 | tf_op args[10]
  5.5 78.5 %ensemble_gradients.1.rz_ref = bf16[8,32,640]{2,1,0:T(8,128)(2,1)} custom-call(bf16[64,1024]{1,0:T(8,128)(2,1)} %bitcast.3, bf16[256,1024]{1,0:T(8,128)(2,1)} %grid_ref.1, s32[256,3]{1,0:T(8,128)} %copy.16.edge_ref, f32[256,100]{1,0:T(8,128)} %copy.17.target_ref, f32[1,256]{1,0:T(1,128)} %bitcast.4, f32[1,100]{1,0:T(1,128)} %bitcast.5, ...), custom_call_target="tpu_custom_call" | custom-call | tf_op jit(solution)/shard_map/ensemble_gradients/pallas_call | solution.py:420
  84.1 1.9 %finish.1 = (f32[32,1024]{1,0:T(8,128)}, f32[32,1024]{1,0:T(8,128)}, f32[32,1024]{1,0:T(8,128)}, f32[32,1024]{1,0:T(8,128)}, f32[32,100]{1,0:T(8,128)}) custom-call(bf16[8,32,640]{2,1,0:T(8,128)(2,1)} %ensemble_gradients.1.rz_ref, bf16[1024,100]{1,0:T(8,128)(2,1)} %copy.18.wh_ref), custom_call_target="tpu_custom_call" | custom-call | tf_op jit(solution)/shard_map/finish/pallas_call | solution.py:432

commit v2 on v1

v2 whole, which is shorter than its diff:
```python
import functools

import jax
import jax.numpy as jnp
from jax import lax
from jax.experimental import pallas as pl
from jax.experimental.pallas import tpu as pltpu
from jax.sharding import PartitionSpec as P

MESH = pl.DeviceIdType.MESH
HEADS = 16
KNN = 3
FAIR_ALPHA = 0.95
SMOOTH_SQ = 0.0625
ENS = 8
SPACE = 32
CX = 4
CY = 4
CHIPS = CX * CY
D = 1024
HD = D // HEADS
G = 256
M = 64
N = 3 * M
E = KNN * G
VAR = 100
VP = 128
C = D // ENS
ROWS = D // SPACE
W = 256
PAIRS = ENS // 2
BF = jnp.bfloat16
F32 = jnp.float32


def dot(a, b):
    return jnp.dot(a, b, preferred_element_type=F32)


def dot_nt(a, b):
    return lax.dot_general(a, b, (((1,), (1,)), ((), ())), preferred_element_type=F32)


def slope(d):
    return d * lax.rsqrt(d * d + SMOOTH_SQ)


def same_head(width, value):
    rows = lax.broadcasted_iota(jnp.int32, (width, width), 0) // HD
    cols = lax.broadcasted_iota(jnp.int32, (width, width), 1) // HD
    return jnp.where(rows == cols, value, 0.0).astype(BF)


def softmax3(scores):
    s0, s1, s2 = scores[:G], scores[G : 2 * G], scores[2 * G :]
    top = jnp.maximum(jnp.maximum(s0, s1), s2)
    e0, e1, e2 = jnp.exp(s0 - top), jnp.exp(s1 - top), jnp.exp(s2 - top)
    inv = 1.0 / (e0 + e1 + e2)
    return e0 * inv, e1 * inv, e2 * inv


def three(x):
    return jnp.concatenate([x, x, x], axis=0)


def side(x, y):
    return jnp.concatenate([x, y], axis=1)


PLACE = {0: 0, -1: 1, 1: 2, -2: 3, 2: 4, -3: 5, 3: 6, -4: 7}


def main_kernel(
    x_ref, grid_ref, edge_ref, target_ref, area_ref, var_ref,
    wq_hbm, wk_hbm, wv_hbm, wo_hbm, wh_ref,
    out_ref,
    wq, wk, wv, wo, wht, lat, lat_t, grid_t, mix_t, q, keys, values, attended, hidden,
    delta, wkvc, kg, vg, att_all, att_low, gl, ga, s_v, s_k, oh, oh_t, q3, gq, uct, common, areaw,
    part_ab, part_v, part_qk, sib_ab, sib_v, sib_qk, sum_ab, sum_v, sum_qk, r_ab, r_v, r_qk, rz,
    wsem, ring_s, ring_r, halo_s, halo_l, halo_r, d_s, d_r, sib_s, sib_r, xy_s, xy_r, z_s, z_r,
):
    e = lax.axis_index("ens")
    s = lax.axis_index("space")
    core = lax.rem(s, 2)
    chip_x = lax.rem(s // 2, CX)
    chip_y = s // (2 * CX)

    loads = [
        pltpu.make_async_copy(src, dst, wsem.at[i])
        for i, (src, dst) in enumerate(((wq_hbm, wq), (wk_hbm, wk), (wv_hbm, wv), (wo_hbm, wo)))
    ]
    for load in loads:
        load.start()

    def ens_peer(d):
        return (lax.rem(e + d + ENS, ENS), s)

    def space_peer(d):
        return (e, lax.rem(s + d + SPACE, SPACE))

    def chip_peer(t):
        return lax.rem(chip_y + t // CX, CY) * CX + lax.rem(chip_x + lax.rem(t, CX), CX)

    sibling = (e, s + 1 - 2 * core)

    barrier = pltpu.get_barrier_semaphore()

    def greet(peer):
        pl.semaphore_signal(barrier, inc=1, device_id=peer, device_id_type=MESH)

    greet(space_peer(1))
    greet(space_peer(-1))

    @pl.loop(1, ENS)
    def _(d):
        greet(ens_peer(d))

    @pl.loop(1, CHIPS)
    def _(t):
        greet((e, chip_peer(t) * 2 + core))

    def own_rows(i):
        return pl.ds(i * N + M, M)

    def ring_copy(d_from, d_to, sem, way):
        return pltpu.make_async_remote_copy(
            src_ref=lat.at[own_rows(PLACE[d_from])], dst_ref=lat.at[own_rows(PLACE[d_to])],
            send_sem=ring_s.at[sem], recv_sem=ring_r.at[PLACE[d_to]],
            device_id=ens_peer(way), device_id_type=MESH,
        )

    forward = {k: ring_copy(1 - k, -k, k - 1, 1) for k in range(1, 5)}
    backward = {k: ring_copy(k - 1, k, 3 + k, -1) for k in range(1, 4)}

    def halo_copies(i):
        up = pltpu.make_async_remote_copy(
            src_ref=lat.at[own_rows(i)], dst_ref=lat.at[pl.ds(i * N, M)],
            send_sem=halo_s.at[i, 0], recv_sem=halo_l.at[i],
            device_id=space_peer(1), device_id_type=MESH,
        )
        down = pltpu.make_async_remote_copy(
            src_ref=lat.at[own_rows(i)], dst_ref=lat.at[pl.ds(i * N + 2 * M, M)],
            send_sem=halo_s.at[i, 1], recv_sem=halo_r.at[i],
            device_id=space_peer(-1), device_id_type=MESH,
        )
        return up, down

    def start_halo(i):
        for copy in halo_copies(i):
            copy.start()

    def wait_halo(i):
        for copy in halo_copies(i):
            copy.wait_recv()

    def arrived(copy, d):
        copy.wait_recv()
        start_halo(PLACE[d])

    lat[own_rows(0), :] = x_ref[...]
    wht[...] = jnp.zeros_like(wht)
    wht[:VAR, :] = wh_ref[...]
    loads[0].wait()
    for n in range(D // W):
        cols = slice(n * W, (n + 1) * W)
        q[:, cols] = dot(grid_ref[...], wq[:, cols]).astype(BF)

    pl.semaphore_wait(barrier, 2 + ENS - 1 + CHIPS - 1)
    start_halo(0)
    forward[1].start()
    backward[1].start()

    edges = edge_ref[...]
    slot_rows = (((edges // M) - s + 1 + SPACE) % SPACE) * M + edges % M
    node = lax.broadcasted_iota(jnp.int32, (N, G), 0)
    for j in range(KNN):
        oh_t[:, j * G : (j + 1) * G] = jnp.where(slot_rows[j : j + 1, :] == node, 1.0, 0.0).astype(BF)
    oh[...] = oh_t[...].T
    grid_t[...] = grid_ref[...].T
    var_row = jnp.concatenate([var_ref[...], jnp.zeros((1, VP - VAR), F32)], axis=1)
    areaw[...] = jnp.broadcast_to(area_ref[...], (VP, G)).T * var_row
    common[...] = dot_nt(grid_ref[...], wht[...])
    for load in loads[1:]:
        load.wait()
    hs = pl.ds(pl.multiple_of(e * C, C), C)
    wkvc[:, :C] = wk[:, hs]
    wkvc[:, C:] = wv[:, hs]
    uct[...] = dot_nt(wht[...], wo[hs, :]).astype(BF)
    q3[...] = three(side(q[:, hs], q[:, hs]))

    wait_halo(0)
    for n in range(D // W):
        cols = slice(n * W, (n + 1) * W)
        keys[:, cols] = dot(lat[:N, :], wk[:, cols]).astype(BF)
        values[:, cols] = dot(lat[:N, :], wv[:, cols]).astype(BF)

    arrived(forward[1], -1)
    arrived(backward[1], 1)
    forward[2].start()
    backward[2].start()

    head_sum = same_head(W, HD**-0.5)
    for n in range(D // W):
        cols = slice(n * W, (n + 1) * W)
        prod = dot(oh[...], keys[:, cols]).astype(BF) * three(q[:, cols])
        att = softmax3(dot(prod, head_sum))
        value_rows = dot(oh[...], values[:, cols])
        total = jnp.zeros((G, W), F32)
        for j in range(KNN):
            total += att[j].astype(BF).astype(F32) * value_rows[j * G : (j + 1) * G]
        attended[:, cols] = total.astype(BF)

    for n in range(D // W):
        cols = slice(n * W, (n + 1) * W)
        update = dot(attended[...], wo[:, cols])
        hidden[:, cols] = (grid_ref[:, cols].astype(F32) + update).astype(BF)

    delta[0] = (dot_nt(hidden[...], wht[...]) - common[...]).astype(BF)

    def delta_copy(d):
        place = PLACE[-d if d <= ENS // 2 else ENS - d]
        return pltpu.make_async_remote_copy(
            src_ref=delta.at[0], dst_ref=delta.at[place],
            send_sem=d_s.at[d], recv_sem=d_r.at[place],
            device_id=ens_peer(d), device_id_type=MESH,
        )

    for d in (4, 3, 5, 2, 6, 1, 7):
        delta_copy(d).start()

    def prepare(p):
        rows = slice(2 * p * N, 2 * (p + 1) * N)
        kv = dot(lat[rows, :], wkvc[...]).astype(BF)
        kg[p] = dot(oh[...], side(kv[:N, :C], kv[N:, :C])).astype(BF)
        vg[p] = dot(oh[...], side(kv[:N, C:], kv[N:, C:])).astype(BF)
        att = softmax3(dot(kg[p] * q3[...], head_sum))
        for j in range(KNN):
            att_all[p, j * G : (j + 1) * G, :] = att[j]
            att_low[p, j * G : (j + 1) * G, :] = att[j].astype(BF)
        lat_t[:, rows] = lat[rows, :].T

    arrived(forward[2], -2)
    arrived(backward[2], 2)
    forward[3].start()
    backward[3].start()
    wait_halo(1)
    prepare(0)
    padded = jnp.concatenate([target_ref[...], jnp.zeros((VP - VAR, G), F32)], axis=0)
    common[...] = common[...] - padded.T
    arrived(forward[3], -3)
    arrived(backward[3], 3)
    forward[4].start()
    wait_halo(2)
    wait_halo(3)
    prepare(1)
    mix_t[:D, :] = attended[...].T
    mix_t[D:, :] = hidden[...].T
    wait_halo(4)
    wait_halo(5)
    prepare(2)
    arrived(forward[4], -4)
    wait_halo(6)
    wait_halo(7)
    prepare(3)

    for d in range(1, ENS):
        delta_copy(d).wait_recv()

    fair_eps = (1.0 - FAIR_ALPHA) / ENS
    pair_coef = (1.0 - fair_eps) / (ENS * (ENS - 1))
    step_rows = 16

    @pl.loop(0, G // step_rows)
    def _(i):
        rows = pl.ds(pl.multiple_of(i * step_rows, step_rows), step_rows)
        dev = [delta[m, rows, :].astype(F32) for m in range(ENS)]
        pair = [None] * ENS
        for a in range(ENS):
            for b in range(a + 1, ENS):
                t = slope(dev[a] - dev[b])
                pair[a] = t if pair[a] is None else pair[a] + t
                pair[b] = -t if pair[b] is None else pair[b] - t
        shift = common[rows, :]
        scale = areaw[rows, :]
        for m in range(ENS):
            grad = scale * (slope(dev[m] + shift) * (1.0 / ENS) - pair_coef * pair[m])
            gl[pl.ds(pl.multiple_of(m * G + i * step_rows, step_rows), step_rows), :] = grad.astype(BF)

    def sibling_copy(i, part, sib):
        return pltpu.make_async_remote_copy(
            src_ref=part.at[1 - core], dst_ref=sib, send_sem=sib_s.at[i], recv_sem=sib_r.at[i],
            device_id=sibling, device_id_type=MESH,
        )

    def chip_copy(i, summed, r, t):
        chip = chip_peer(t)
        return pltpu.make_async_remote_copy(
            src_ref=summed.at[pl.ds(pl.multiple_of(chip * ROWS, ROWS), ROWS)], dst_ref=r.at[t],
            send_sem=xy_s.at[i, t], recv_sem=xy_r.at[i, t],
            device_id=(e, chip * 2 + core), device_id_type=MESH,
        )

    def spread(i, part, sib, summed, r):
        sibling_copy(i, part, sib).wait_recv()
        summed[...] = (part[core].astype(F32) + sib[...].astype(F32)).astype(BF)

        @pl.loop(1, CHIPS)
        def _(t):
            chip_copy(i, summed, r, t).start()

        r[0] = summed[pl.ds(pl.multiple_of((s // 2) * ROWS, ROWS), ROWS), :]

    def last_copy(i, cols, d, m):
        return pltpu.make_async_remote_copy(
            src_ref=rz.at[e, :, cols], dst_ref=rz.at[m, :, cols],
            send_sem=z_s.at[i, d], recv_sem=z_r.at[i, m],
            device_id=ens_peer(d), device_id_type=MESH,
        )

    def collect(i, summed, r, cols):
        @pl.loop(1, CHIPS)
        def _(t):
            chip_copy(i, summed, r, t).wait_recv()

        rz[e, :, cols] = jnp.sum(r[...].astype(F32), axis=0).astype(BF)

        @pl.loop(1, ENS)
        def _(d):
            last_copy(i, cols, d, e).start()

    def put(part, chunk, cols, value):
        value = value.astype(BF)
        for k in range(W // ROWS):
            dest = chunk * (W // ROWS) + k
            rows = slice((dest // 2) * ROWS, (dest // 2 + 1) * ROWS)
            part[dest % 2, rows, cols] = value[k * ROWS : (k + 1) * ROWS, :]

    ab, v, qk = (0, part_ab, sib_ab), (1, part_v, sib_v), (2, part_qk, sib_qk)
    for i in range(D // W):
        rows = slice(i * W, (i + 1) * W)
        put(part_ab, i, slice(0, VP), dot(mix_t[rows, :], gl[:G, :]))
        put(part_ab, i, slice(VP, 2 * VP), dot(mix_t[D + i * W : D + (i + 1) * W, :], gl[:G, :]))
    sibling_copy(*ab).start()

    @pl.loop(0, ENS // 2)
    def _(p):
        rows = pl.ds(pl.multiple_of(p * 2 * G, 2 * G), 2 * G)
        both = dot(gl[rows, :], uct[...]).astype(BF)
        both = side(both[:G], both[G:])
        ga[p] = both
        sums = dot(oh_t[...], att_low[p] * three(both)).astype(BF)
        s_v[pl.ds(pl.multiple_of(p * 2 * N, N), N), :] = sums[:, :C]
        s_v[pl.ds(pl.multiple_of(p * 2 * N + N, N), N), :] = sums[:, C:]

    for i in range(D // W):
        put(part_v, i, slice(0, C), dot(lat_t[i * W : (i + 1) * W, :], s_v[...]))
    sibling_copy(*v).start()
    spread(*ab, sum_ab, r_ab)

    gq[...] = jnp.zeros_like(gq)
    ones = same_head(W, 1.0)

    @pl.loop(0, ENS // 2)
    def _(p):
        gw = dot(vg[p] * three(ga[p]), ones)
        att = att_all[p]
        t = att * gw
        gs = (att * (gw - three(t[:G] + t[G : 2 * G] + t[2 * G :])) * HD**-0.5).astype(BF)
        gqe = gs.astype(F32) * kg[p].astype(F32)
        gqe = gqe[:G] + gqe[G : 2 * G] + gqe[2 * G :]
        gq[...] += gqe[:, :C] + gqe[:, C:]
        sums = dot(oh_t[...], gs * q3[...]).astype(BF)
        s_k[pl.ds(pl.multiple_of(p * 2 * N, N), N), :] = sums[:, :C]
        s_k[pl.ds(pl.multiple_of(p * 2 * N + N, N), N), :] = sums[:, C:]

    spread(*v, sum_v, r_v)
    for i in range(D // W):
        rows = slice(i * W, (i + 1) * W)
        put(part_qk, i, slice(0, C), dot(grid_t[rows, :], gq[...].astype(BF)))
        put(part_qk, i, slice(C, 2 * C), dot(lat_t[rows, :], s_k[...]))
    sibling_copy(*qk).start()
    qk_cols, v_cols, ab_cols = slice(0, 2 * C), slice(2 * C, 3 * C), slice(3 * C, 3 * C + 2 * VP)
    collect(0, sum_ab, r_ab, ab_cols)
    spread(*qk, sum_qk, r_qk)
    collect(1, sum_v, r_v, v_cols)
    collect(2, sum_qk, r_qk, qk_cols)

    for copy in [*forward.values(), *backward.values()]:
        copy.wait_send()
    for i in range(ENS):
        for copy in halo_copies(i):
            copy.wait_send()
    for d in range(1, ENS):
        delta_copy(d).wait_send()
    for i, summed, r, cols in ((0, sum_ab, r_ab, ab_cols), (1, sum_v, r_v, v_cols), (2, sum_qk, r_qk, qk_cols)):
        sibling_copy(*(ab, v, qk)[i]).wait_send()

        @pl.loop(1, CHIPS)
        def _(t, i=i, summed=summed, r=r):
            chip_copy(i, summed, r, t).wait_send()

        @pl.loop(1, ENS)
        def _(d, i=i, cols=cols):
            last_copy(i, cols, d, e).wait_send()
            last_copy(i, cols, d, lax.rem(e + d, ENS)).wait_recv()

    out_ref[...] = rz[...]


def finish_kernel(rz_ref, wh_ref, q_ref, k_ref, v_ref, p_ref, h_ref):
    for m in range(ENS):
        cols = slice(m * C, (m + 1) * C)
        q_ref[:, cols] = rz_ref[m, :, :C].astype(F32)
        k_ref[:, cols] = rz_ref[m, :, C : 2 * C].astype(F32)
        v_ref[:, cols] = rz_ref[m, :, 2 * C : 3 * C].astype(F32)
    mixed = rz_ref[0, :, 3 * C :].astype(F32)
    for m in range(1, ENS):
        mixed += rz_ref[m, :, 3 * C :].astype(F32)
    h_ref[...] = mixed[:, VP : VP + VAR]
    p_ref[...] = dot(mixed[:, :VAR].astype(BF), wh_ref[...])


def local(x, grid, edges, target, area, var, wq, wk, wv, wo, wh):
    vmem = pl.BlockSpec(memory_space=pltpu.VMEM)
    anywhere = pl.BlockSpec(memory_space=pl.ANY)
    dma = pltpu.SemaphoreType.DMA
    widths = (2 * VP, C, 2 * C)
    scratch = [
        *[pltpu.VMEM((D, D), BF)] * 4,
        pltpu.VMEM((VP, D), BF),
        pltpu.VMEM((ENS * N, D), BF), pltpu.VMEM((D, ENS * N), BF),
        pltpu.VMEM((D, G), BF), pltpu.VMEM((2 * D, G), BF),
        pltpu.VMEM((G, D), BF), pltpu.VMEM((N, D), BF), pltpu.VMEM((N, D), BF),
        pltpu.VMEM((G, D), BF), pltpu.VMEM((G, D), BF),
        pltpu.VMEM((ENS, G, VP), BF), pltpu.VMEM((D, 2 * C), BF),
        pltpu.VMEM((PAIRS, E, W), BF), pltpu.VMEM((PAIRS, E, W), BF),
        pltpu.VMEM((PAIRS, E, W), F32), pltpu.VMEM((PAIRS, E, W), BF),
        pltpu.VMEM((ENS * G, VP), BF), pltpu.VMEM((PAIRS, G, W), BF),
        pltpu.VMEM((ENS * N, C), BF), pltpu.VMEM((ENS * N, C), BF),
        pltpu.VMEM((E, N), BF), pltpu.VMEM((N, E), BF),
        pltpu.VMEM((E, W), BF), pltpu.VMEM((G, C), F32), pltpu.VMEM((VP, C), BF),
        pltpu.VMEM((G, VP), F32), pltpu.VMEM((G, VP), F32),
        *[pltpu.VMEM((2, D // 2, w), BF) for w in widths],
        *[pltpu.VMEM((D // 2, w), BF) for w in widths],
        *[pltpu.VMEM((D // 2, w), BF) for w in widths],
        *[pltpu.VMEM((CHIPS, ROWS, w), BF) for w in widths],
        pltpu.VMEM((ENS, ROWS, 3 * C + 2 * VP), BF),
        dma((4,)), dma((7,)), dma((ENS,)), dma((ENS, 2)), dma((ENS,)), dma((ENS,)),
        dma((ENS,)), dma((ENS,)), dma((3,)), dma((3,)), dma((3, CHIPS)), dma((3, CHIPS)),
        dma((3, ENS)), dma((3, ENS)),
    ]
    rz = pl.pallas_call(
        main_kernel,
        out_shape=jax.ShapeDtypeStruct((ENS, ROWS, 3 * C + 2 * VP), BF),
        in_specs=[vmem] * 6 + [anywhere] * 4 + [vmem],
        out_specs=vmem,
        scratch_shapes=scratch,
        compiler_params=pltpu.CompilerParams(
            collective_id=0, has_side_effects=True, vmem_limit_bytes=56 << 20
        ),
        name="ensemble_gradients",
    )(x[0], grid, edges.T, target.T, area.reshape(1, G), var.reshape(1, VAR), wq, wk, wv, wo, wh.T)
    full = jax.ShapeDtypeStruct((ROWS, D), F32)
    return pl.pallas_call(
        finish_kernel,
        out_shape=(full, full, full, full, jax.ShapeDtypeStruct((ROWS, VAR), F32)),
        in_specs=[vmem, vmem],
        out_specs=(vmem,) * 5,
        name="finish",
    )(rz, wh.T)


def solution(mesh):
    in_specs = (
        P("ens", "space", None),
        P("space", None),
        P("space", None),
        P("space", None),
        P("space"),
        P(),
        P(),
        P(),
        P(),
        P(),
        P(),
    )
    out_specs = (P("space", None),) * 5
    return jax.shard_map(local, mesh=mesh, in_specs=in_specs, out_specs=out_specs, check_vma=False)
```

time: 86.2 us -> 74.5 us (0.86)
  Pallas kernels: 80.5 us -> 73.7 us
  local copies, waits for them, and re-layouts: 4.91 us -> 0 us
    pallas_call x1, Pallas kernels: 78.5 us -> 71.9 us  [local(): pl.pallas_call(main_kernel, out_shape=jax.ShapeDtypeStruct((ENS, ROWS, 3...]
    unnamed x3 -> x0, local copies, waits for them, and re-layouts: 4.91 us -> none
where the time goes in v2:
time: 74.5 us; the launch traced here: 74.4 us
  Pallas kernels  73.7 us (99%)
    pallas_call x1, Pallas kernels, local(): pl.pallas_call(main_kernel, out_shape=jax.ShapeDtypeStruct((ENS, ROWS, 3...  71.9 us
    pallas_call x1, Pallas kernels, local(): pl.pallas_call(finish_kernel, out_shape=(full, full, full, full, jax.Shap...  1.86 us

profile of v2, /device:TPU:1, one launch (start us, length us, event | category | flops | bytes accessed | tf_op | source)
XLA Modules:
  0.0 74.4 jit_solution(4221355209935040659)
XLA Ops:
  0.6 71.9 %ensemble_gradients.1.rz_ref = bf16[8,32,640]{2,1,0:T(8,128)(2,1)} custom-call(bf16[64,1024]{1,0:T(8,128)(2,1)} %bitcast.8, bf16[256,1024]{1,0:T(8,128)(2,1)} %grid_ref.1, s32[3,256]{1,0:T(4,128)} %bitcast.10, f32[100,256]{1,0:T(8,128)} %bitcast.9, f32[1,256]{1,0:T(1,128)} %bitcast.11, f32[1,100]{1,0:T(1,128)} %bitcast.12, bf16[1024,1024]{1,0:T(8,128)(2,1)} %wq_hbm.1, ...), custom_call_target="tpu_custom_call" | custom-call | tf_op jit(solution)/shard_map/ensemble_gradients/pallas_call | solution.py:452
  72.5 1.9 %finish.1 = (f32[32,1024]{1,0:T(8,128)}, f32[32,1024]{1,0:T(8,128)}, f32[32,1024]{1,0:T(8,128)}, f32[32,1024]{1,0:T(8,128)}, f32[32,100]{1,0:T(8,128)}) custom-call(bf16[8,32,640]{2,1,0:T(8,128)(2,1)} %ensemble_gradients.1.rz_ref, bf16[100,1024]{1,0:T(8,128)(2,1)} %bitcast.7), custom_call_target="tpu_custom_call" | custom-call | tf_op jit(solution)/shard_map/finish/pallas_call | solution.py:464

commit v3 on v2

--- a/solution.py
+++ b/solution.py
@@ -67,14 +67,14 @@
     return jnp.concatenate([x, y], axis=1)
 
 
-PLACE = {0: 0, -1: 1, 1: 2, -2: 3, 2: 4, -3: 5, 3: 6, -4: 7}
+PLACE = {0: 0, -1: 1, 1: 2, -2: 3, 2: 4, -3: 5, 3: 6, -4: 7, 4: 7}
 
 
 def main_kernel(
-    x_ref, grid_ref, edge_ref, target_ref, area_ref, var_ref,
-    wq_hbm, wk_hbm, wv_hbm, wo_hbm, wh_ref,
-    out_ref,
-    wq, wk, wv, wo, wht, lat, lat_t, grid_t, mix_t, q, keys, values, attended, hidden,
+    x_hbm, grid_hbm, edge_ref, target_hbm, area_ref, var_ref,
+    wq_hbm, wk_hbm, wv_hbm, wo_hbm, wh_hbm,
+    out_hbm,
+    grid_ref, target_ref, wh_ref, wq, wk, wv, wo, wht, lat, lat_t, grid_t, mix_t, q, keys, values, attended, hidden,
     delta, wkvc, kg, vg, att_all, att_low, gl, ga, s_v, s_k, oh, oh_t, q3, gq, uct, common, areaw,
     part_ab, part_v, part_qk, sib_ab, sib_v, sib_qk, sum_ab, sum_v, sum_qk, r_ab, r_v, r_qk, rz,
     wsem, ring_s, ring_r, halo_s, halo_l, halo_r, d_s, d_r, sib_s, sib_r, xy_s, xy_r, z_s, z_r,
@@ -85,13 +85,6 @@
     chip_x = lax.rem(s // 2, CX)
     chip_y = s // (2 * CX)
 
-    loads = [
-        pltpu.make_async_copy(src, dst, wsem.at[i])
-        for i, (src, dst) in enumerate(((wq_hbm, wq), (wk_hbm, wk), (wv_hbm, wv), (wo_hbm, wo)))
-    ]
-    for load in loads:
-        load.start()
-
     def ens_peer(d):
         return (lax.rem(e + d + ENS, ENS), s)
 
@@ -122,15 +115,34 @@
     def own_rows(i):
         return pl.ds(i * N + M, M)
 
+    def load(i, src, dst):
+        copy = pltpu.make_async_copy(src, dst, wsem.at[i])
+        copy.start()
+        return copy
+
+    load_x = load(0, x_hbm, lat.at[own_rows(0)])
+    load_grid = load(1, grid_hbm, grid_ref)
+    load_wq = load(2, wq_hbm, wq)
+    loads = [
+        load(i + 3, src, dst)
+        for i, (src, dst) in enumerate(
+            ((wh_hbm, wh_ref), (wk_hbm, wk), (wv_hbm, wv), (wo_hbm, wo), (target_hbm, target_ref))
+        )
+    ]
+
     def ring_copy(d_from, d_to, sem, way):
+        src, dst = own_rows(PLACE[d_from]), own_rows(PLACE[d_to])
+        if abs(d_to) == ENS // 2:
+            half = 0 if way > 0 else M // 2
+            src = pl.ds(PLACE[d_from] * N + M + half, M // 2)
+            dst = pl.ds(PLACE[-4] * N + M + half, M // 2)
         return pltpu.make_async_remote_copy(
-            src_ref=lat.at[own_rows(PLACE[d_from])], dst_ref=lat.at[own_rows(PLACE[d_to])],
-            send_sem=ring_s.at[sem], recv_sem=ring_r.at[PLACE[d_to]],
+            src_ref=lat.at[src], dst_ref=lat.at[dst], send_sem=ring_s.at[sem], recv_sem=ring_r.at[sem],
             device_id=ens_peer(way), device_id_type=MESH,
         )
 
     forward = {k: ring_copy(1 - k, -k, k - 1, 1) for k in range(1, 5)}
-    backward = {k: ring_copy(k - 1, k, 3 + k, -1) for k in range(1, 4)}
+    backward = {k: ring_copy(k - 1, k, 3 + k, -1) for k in range(1, 5)}
 
     def halo_copies(i):
         up = pltpu.make_async_remote_copy(
@@ -157,19 +169,22 @@
         copy.wait_recv()
         start_halo(PLACE[d])
 
-    lat[own_rows(0), :] = x_ref[...]
-    wht[...] = jnp.zeros_like(wht)
-    wht[:VAR, :] = wh_ref[...]
-    loads[0].wait()
+    load_grid.wait()
+    load_wq.wait()
     for n in range(D // W):
         cols = slice(n * W, (n + 1) * W)
         q[:, cols] = dot(grid_ref[...], wq[:, cols]).astype(BF)
 
+    load_x.wait()
     pl.semaphore_wait(barrier, 2 + ENS - 1 + CHIPS - 1)
     start_halo(0)
     forward[1].start()
     backward[1].start()
 
+    for copy in loads:
+        copy.wait()
+    wht[...] = jnp.zeros_like(wht)
+    wht[:VAR, :] = wh_ref[...]
     edges = edge_ref[...]
     slot_rows = (((edges // M) - s + 1 + SPACE) % SPACE) * M + edges % M
     node = lax.broadcasted_iota(jnp.int32, (N, G), 0)
@@ -180,8 +195,6 @@
     var_row = jnp.concatenate([var_ref[...], jnp.zeros((1, VP - VAR), F32)], axis=1)
     areaw[...] = jnp.broadcast_to(area_ref[...], (VP, G)).T * var_row
     common[...] = dot_nt(grid_ref[...], wht[...])
-    for load in loads[1:]:
-        load.wait()
     hs = pl.ds(pl.multiple_of(e * C, C), C)
     wkvc[:, :C] = wk[:, hs]
     wkvc[:, C:] = wv[:, hs]
@@ -217,16 +230,20 @@
 
     delta[0] = (dot_nt(hidden[...], wht[...]) - common[...]).astype(BF)
 
-    def delta_copy(d):
-        place = PLACE[-d if d <= ENS // 2 else ENS - d]
+    def delta_copy(sem, d_from, d_to, way, rows=slice(None)):
         return pltpu.make_async_remote_copy(
-            src_ref=delta.at[0], dst_ref=delta.at[place],
-            send_sem=d_s.at[d], recv_sem=d_r.at[place],
-            device_id=ens_peer(d), device_id_type=MESH,
-        )
-
-    for d in (4, 3, 5, 2, 6, 1, 7):
-        delta_copy(d).start()
+            src_ref=delta.at[PLACE[d_from], rows], dst_ref=delta.at[PLACE[d_to], rows],
+            send_sem=d_s.at[sem], recv_sem=d_r.at[sem],
+            device_id=ens_peer(way), device_id_type=MESH,
+        )
+
+    near = [delta_copy(0, 0, -2, 2), delta_copy(1, 0, 2, -2), delta_copy(2, 0, -1, 1), delta_copy(3, 0, 1, -1)]
+    far = [
+        delta_copy(4, -2, -4, 2, pl.ds(0, G // 2)), delta_copy(5, 2, -4, -2, pl.ds(G // 2, G // 2)),
+        delta_copy(6, -2, -3, 1), delta_copy(7, 2, 3, -1),
+    ]
+    for copy in near:
+        copy.start()
 
     def prepare(p):
         rows = slice(2 * p * N, 2 * (p + 1) * N)
@@ -245,11 +262,16 @@
     backward[3].start()
     wait_halo(1)
     prepare(0)
+    near[0].wait_recv()
+    near[1].wait_recv()
+    for copy in far:
+        copy.start()
     padded = jnp.concatenate([target_ref[...], jnp.zeros((VP - VAR, G), F32)], axis=0)
     common[...] = common[...] - padded.T
     arrived(forward[3], -3)
     arrived(backward[3], 3)
     forward[4].start()
+    backward[4].start()
     wait_halo(2)
     wait_halo(3)
     prepare(1)
@@ -258,13 +280,14 @@
     wait_halo(4)
     wait_halo(5)
     prepare(2)
+    backward[4].wait_recv()
     arrived(forward[4], -4)
     wait_halo(6)
     wait_halo(7)
     prepare(3)
 
-    for d in range(1, ENS):
-        delta_copy(d).wait_recv()
+    for copy in [*near[2:], *far]:
+        copy.wait_recv()
 
     fair_eps = (1.0 - FAIR_ALPHA) / ENS
     pair_coef = (1.0 - fair_eps) / (ENS * (ENS - 1))
@@ -380,18 +403,17 @@
         put(part_qk, i, slice(C, 2 * C), dot(lat_t[rows, :], s_k[...]))
     sibling_copy(*qk).start()
     qk_cols, v_cols, ab_cols = slice(0, 2 * C), slice(2 * C, 3 * C), slice(3 * C, 3 * C + 2 * VP)
+    spread(*qk, sum_qk, r_qk)
     collect(0, sum_ab, r_ab, ab_cols)
-    spread(*qk, sum_qk, r_qk)
     collect(1, sum_v, r_v, v_cols)
     collect(2, sum_qk, r_qk, qk_cols)
 
-    for copy in [*forward.values(), *backward.values()]:
+    for copy in [*forward.values(), *backward.values(), *near, *far]:
         copy.wait_send()
     for i in range(ENS):
         for copy in halo_copies(i):
             copy.wait_send()
-    for d in range(1, ENS):
-        delta_copy(d).wait_send()
+    stores = []
     for i, summed, r, cols in ((0, sum_ab, r_ab, ab_cols), (1, sum_v, r_v, v_cols), (2, sum_qk, r_qk, qk_cols)):
         sibling_copy(*(ab, v, qk)[i]).wait_send()
 
@@ -404,7 +426,10 @@
             last_copy(i, cols, d, e).wait_send()
             last_copy(i, cols, d, lax.rem(e + d, ENS)).wait_recv()
 
-    out_ref[...] = rz[...]
+        stores.append(pltpu.make_async_copy(rz.at[:, :, cols], out_hbm.at[:, :, cols], wsem.at[i]))
+        stores[-1].start()
+    for store in stores:
+        store.wait()
 
 
 def finish_kernel(rz_ref, wh_ref, q_ref, k_ref, v_ref, p_ref, h_ref):
@@ -426,6 +451,7 @@
     dma = pltpu.SemaphoreType.DMA
     widths = (2 * VP, C, 2 * C)
     scratch = [
+        pltpu.VMEM((G, D), BF), pltpu.VMEM((VAR, G), F32), pltpu.VMEM((VAR, D), BF),
         *[pltpu.VMEM((D, D), BF)] * 4,
         pltpu.VMEM((VP, D), BF),
         pltpu.VMEM((ENS * N, D), BF), pltpu.VMEM((D, ENS * N), BF),
@@ -445,15 +471,15 @@
         *[pltpu.VMEM((D // 2, w), BF) for w in widths],
         *[pltpu.VMEM((CHIPS, ROWS, w), BF) for w in widths],
         pltpu.VMEM((ENS, ROWS, 3 * C + 2 * VP), BF),
-        dma((4,)), dma((7,)), dma((ENS,)), dma((ENS, 2)), dma((ENS,)), dma((ENS,)),
+        dma((8,)), dma((8,)), dma((8,)), dma((ENS, 2)), dma((ENS,)), dma((ENS,)),
         dma((ENS,)), dma((ENS,)), dma((3,)), dma((3,)), dma((3, CHIPS)), dma((3, CHIPS)),
         dma((3, ENS)), dma((3, ENS)),
     ]
     rz = pl.pallas_call(
         main_kernel,
         out_shape=jax.ShapeDtypeStruct((ENS, ROWS, 3 * C + 2 * VP), BF),
-        in_specs=[vmem] * 6 + [anywhere] * 4 + [vmem],
-        out_specs=vmem,
+        in_specs=[anywhere, anywhere, vmem, anywhere, vmem, vmem] + [anywhere] * 5,
+        out_specs=anywhere,
         scratch_shapes=scratch,
         compiler_params=pltpu.CompilerParams(
             collective_id=0, has_side_effects=True, vmem_limit_bytes=56 << 20

time: 74.5 us -> 68.1 us (0.914)
  Pallas kernels: 73.7 us -> 67.4 us
    pallas_call x1, Pallas kernels: 71.9 us -> 65.5 us  [local(): pl.pallas_call(main_kernel, out_shape=jax.ShapeDtypeStruct((ENS, ROWS, 3...]
where the time goes in v3:
time: 68.1 us; the launch traced here: 68 us
  Pallas kernels  67.4 us (99%)
    pallas_call x1, Pallas kernels, local(): pl.pallas_call(main_kernel, out_shape=jax.ShapeDtypeStruct((ENS, ROWS, 3...  65.5 us
    pallas_call x1, Pallas kernels, local(): pl.pallas_call(finish_kernel, out_shape=(full, full, full, full, jax.Shap...  1.86 us

profile of v3, /device:TPU:1, one launch (start us, length us, event | category | flops | bytes accessed | tf_op | source)
XLA Modules:
  0.0 68.0 jit_solution(11276417178505957066)
XLA Ops:
  0.6 65.5 %ensemble_gradients.1.rz_ref = bf16[8,32,640]{2,1,0:T(8,128)(2,1)} custom-call(bf16[64,1024]{1,0:T(8,128)(2,1)} %bitcast.8, bf16[256,1024]{1,0:T(8,128)(2,1)} %grid_hbm.1, s32[3,256]{1,0:T(4,128)} %bitcast.10, f32[100,256]{1,0:T(8,128)} %bitcast.9, f32[1,256]{1,0:T(1,128)} %bitcast.11, f32[1,100]{1,0:T(1,128)} %bitcast.12, bf16[1024,1024]{1,0:T(8,128)(2,1)} %wq_hbm.1, ...), custom_call_target="tpu_custom_call" | custom-call | tf_op jit(solution)/shard_map/ensemble_gradients/pallas_call | solution.py:478
  66.1 1.9 %finish.1 = (f32[32,1024]{1,0:T(8,128)}, f32[32,1024]{1,0:T(8,128)}, f32[32,1024]{1,0:T(8,128)}, f32[32,1024]{1,0:T(8,128)}, f32[32,100]{1,0:T(8,128)}) custom-call(bf16[8,32,640]{2,1,0:T(8,128)(2,1)} %ensemble_gradients.1.rz_ref, bf16[100,1024]{1,0:T(8,128)(2,1)} %bitcast.7), custom_call_target="tpu_custom_call" | custom-call | tf_op jit(solution)/shard_map/finish/pallas_call | solution.py:490

commit v4 on v3

--- a/solution.py
+++ b/solution.py
@@ -130,19 +130,25 @@
         )
     ]
 
-    def ring_copy(d_from, d_to, sem, way):
-        src, dst = own_rows(PLACE[d_from]), own_rows(PLACE[d_to])
-        if abs(d_to) == ENS // 2:
-            half = 0 if way > 0 else M // 2
-            src = pl.ds(PLACE[d_from] * N + M + half, M // 2)
-            dst = pl.ds(PLACE[-4] * N + M + half, M // 2)
+    def ring_copy(step, way, half):
+        src = pl.ds(PLACE[(1 - step) * way] * N + M + half * (M // 2), M // 2)
+        dst = pl.ds(PLACE[-step * way] * N + M + half * (M // 2), M // 2)
+        sem = (step - 1) * 4 + (1 - way) + half
         return pltpu.make_async_remote_copy(
             src_ref=lat.at[src], dst_ref=lat.at[dst], send_sem=ring_s.at[sem], recv_sem=ring_r.at[sem],
             device_id=ens_peer(way), device_id_type=MESH,
         )
 
-    forward = {k: ring_copy(1 - k, -k, k - 1, 1) for k in range(1, 5)}
-    backward = {k: ring_copy(k - 1, k, 3 + k, -1) for k in range(1, 5)}
+    ring = {(k, w, h): ring_copy(k, w, h) for k in range(1, 4) for h in (0, 1) for w in (1, -1)}
+    ring[4, 1, 0] = ring_copy(4, 1, 0)
+    ring[4, -1, 1] = ring_copy(4, -1, 1)
+
+    def pass_on(step, half):
+        for way in (1, -1):
+            if (step, way, half) in ring:
+                ring[step, way, half].wait_recv()
+            if (step + 1, way, half) in ring:
+                ring[step + 1, way, half].start()
 
     def halo_copies(i):
         up = pltpu.make_async_remote_copy(
@@ -165,10 +171,6 @@
         for copy in halo_copies(i):
             copy.wait_recv()
 
-    def arrived(copy, d):
-        copy.wait_recv()
-        start_halo(PLACE[d])
-
     load_grid.wait()
     load_wq.wait()
     for n in range(D // W):
@@ -178,8 +180,9 @@
     load_x.wait()
     pl.semaphore_wait(barrier, 2 + ENS - 1 + CHIPS - 1)
     start_halo(0)
-    forward[1].start()
-    backward[1].start()
+    for half in (0, 1):
+        ring[1, 1, half].start()
+        ring[1, -1, half].start()
 
     for copy in loads:
         copy.wait()
@@ -202,15 +205,15 @@
     q3[...] = three(side(q[:, hs], q[:, hs]))
 
     wait_halo(0)
+    pass_on(1, 0)
     for n in range(D // W):
         cols = slice(n * W, (n + 1) * W)
         keys[:, cols] = dot(lat[:N, :], wk[:, cols]).astype(BF)
         values[:, cols] = dot(lat[:N, :], wv[:, cols]).astype(BF)
-
-    arrived(forward[1], -1)
-    arrived(backward[1], 1)
-    forward[2].start()
-    backward[2].start()
+        if n == 1:
+            pass_on(1, 1)
+            start_halo(PLACE[-1])
+            start_halo(PLACE[1])
 
     head_sum = same_head(W, HD**-0.5)
     for n in range(D // W):
@@ -222,7 +225,12 @@
         for j in range(KNN):
             total += att[j].astype(BF).astype(F32) * value_rows[j * G : (j + 1) * G]
         attended[:, cols] = total.astype(BF)
-
+        if n == 1:
+            pass_on(2, 0)
+
+    pass_on(2, 1)
+    start_halo(PLACE[-2])
+    start_halo(PLACE[2])
     for n in range(D // W):
         cols = slice(n * W, (n + 1) * W)
         update = dot(attended[...], wo[:, cols])
@@ -237,13 +245,21 @@
             device_id=ens_peer(way), device_id_type=MESH,
         )
 
-    near = [delta_copy(0, 0, -2, 2), delta_copy(1, 0, 2, -2), delta_copy(2, 0, -1, 1), delta_copy(3, 0, 1, -1)]
-    far = [
-        delta_copy(4, -2, -4, 2, pl.ds(0, G // 2)), delta_copy(5, 2, -4, -2, pl.ds(G // 2, G // 2)),
-        delta_copy(6, -2, -3, 1), delta_copy(7, 2, 3, -1),
-    ]
-    for copy in near:
+    halves = (pl.ds(0, G // 2), pl.ds(G // 2, G // 2))
+    near2 = {(w, h): delta_copy(1 - w + h, 0, -2 * w, 2 * w, halves[h]) for h in (0, 1) for w in (1, -1)}
+    near1 = {w: delta_copy(4 + (1 - w) // 2, 0, -w, w) for w in (1, -1)}
+    far3 = {(w, h): delta_copy(6 + 1 - w + h, -2 * w, -3 * w, w, halves[h]) for h in (0, 1) for w in (1, -1)}
+    far4 = {w: delta_copy(10 + (1 - w) // 2, -2 * w, 4, 2 * w, halves[(1 - w) // 2]) for w in (1, -1)}
+    deltas = [*near2.values(), *near1.values(), *far3.values(), *far4.values()]
+    for copy in [*near2.values(), *near1.values()]:
         copy.start()
+
+    def pass_delta_on(half):
+        for way in (1, -1):
+            near2[way, half].wait_recv()
+            if half == (1 - way) // 2:
+                far4[way].start()
+            far3[way, half].start()
 
     def prepare(p):
         rows = slice(2 * p * N, 2 * (p + 1) * N)
@@ -256,37 +272,32 @@
             att_low[p, j * G : (j + 1) * G, :] = att[j].astype(BF)
         lat_t[:, rows] = lat[rows, :].T
 
-    arrived(forward[2], -2)
-    arrived(backward[2], 2)
-    forward[3].start()
-    backward[3].start()
+    padded = jnp.concatenate([target_ref[...], jnp.zeros((VP - VAR, G), F32)], axis=0)
+    common[...] = common[...] - padded.T
+    mix_t[:D, :] = attended[...].T
+    pass_on(3, 0)
     wait_halo(1)
     prepare(0)
-    near[0].wait_recv()
-    near[1].wait_recv()
-    for copy in far:
-        copy.start()
-    padded = jnp.concatenate([target_ref[...], jnp.zeros((VP - VAR, G), F32)], axis=0)
-    common[...] = common[...] - padded.T
-    arrived(forward[3], -3)
-    arrived(backward[3], 3)
-    forward[4].start()
-    backward[4].start()
+    pass_on(3, 1)
+    start_halo(PLACE[-3])
+    start_halo(PLACE[3])
+    mix_t[D:, :] = hidden[...].T
+    pass_delta_on(0)
     wait_halo(2)
     wait_halo(3)
     prepare(1)
-    mix_t[:D, :] = attended[...].T
-    mix_t[D:, :] = hidden[...].T
+    pass_delta_on(1)
+    pass_on(4, 0)
+    pass_on(4, 1)
+    start_halo(PLACE[4])
     wait_halo(4)
     wait_halo(5)
     prepare(2)
-    backward[4].wait_recv()
-    arrived(forward[4], -4)
     wait_halo(6)
     wait_halo(7)
     prepare(3)
 
-    for copy in [*near[2:], *far]:
+    for copy in [*near1.values(), *far3.values(), *far4.values()]:
         copy.wait_recv()
 
     fair_eps = (1.0 - FAIR_ALPHA) / ENS
@@ -347,8 +358,7 @@
 
         rz[e, :, cols] = jnp.sum(r[...].astype(F32), axis=0).astype(BF)
 
-        @pl.loop(1, ENS)
-        def _(d):
+        for d in (4, 3, 5, 2, 6, 1, 7):
             last_copy(i, cols, d, e).start()
 
     def put(part, chunk, cols, value):
@@ -365,15 +375,14 @@
         put(part_ab, i, slice(VP, 2 * VP), dot(mix_t[D + i * W : D + (i + 1) * W, :], gl[:G, :]))
     sibling_copy(*ab).start()
 
-    @pl.loop(0, ENS // 2)
-    def _(p):
-        rows = pl.ds(pl.multiple_of(p * 2 * G, 2 * G), 2 * G)
+    for p in range(PAIRS):
+        rows = slice(p * 2 * G, (p + 1) * 2 * G)
         both = dot(gl[rows, :], uct[...]).astype(BF)
         both = side(both[:G], both[G:])
         ga[p] = both
         sums = dot(oh_t[...], att_low[p] * three(both)).astype(BF)
-        s_v[pl.ds(pl.multiple_of(p * 2 * N, N), N), :] = sums[:, :C]
-        s_v[pl.ds(pl.multiple_of(p * 2 * N + N, N), N), :] = sums[:, C:]
+        s_v[2 * p * N : (2 * p + 1) * N, :] = sums[:, :C]
+        s_v[(2 * p + 1) * N : (2 * p + 2) * N, :] = sums[:, C:]
 
     for i in range(D // W):
         put(part_v, i, slice(0, C), dot(lat_t[i * W : (i + 1) * W, :], s_v[...]))
@@ -383,8 +392,7 @@
     gq[...] = jnp.zeros_like(gq)
     ones = same_head(W, 1.0)
 
-    @pl.loop(0, ENS // 2)
-    def _(p):
+    for p in range(PAIRS):
         gw = dot(vg[p] * three(ga[p]), ones)
         att = att_all[p]
         t = att * gw
@@ -393,8 +401,8 @@
         gqe = gqe[:G] + gqe[G : 2 * G] + gqe[2 * G :]
         gq[...] += gqe[:, :C] + gqe[:, C:]
         sums = dot(oh_t[...], gs * q3[...]).astype(BF)
-        s_k[pl.ds(pl.multiple_of(p * 2 * N, N), N), :] = sums[:, :C]
-        s_k[pl.ds(pl.multiple_of(p * 2 * N + N, N), N), :] = sums[:, C:]
+        s_k[2 * p * N : (2 * p + 1) * N, :] = sums[:, :C]
+        s_k[(2 * p + 1) * N : (2 * p + 2) * N, :] = sums[:, C:]
 
     spread(*v, sum_v, r_v)
     for i in range(D // W):
@@ -408,7 +416,7 @@
     collect(1, sum_v, r_v, v_cols)
     collect(2, sum_qk, r_qk, qk_cols)
 
-    for copy in [*forward.values(), *backward.values(), *near, *far]:
+    for copy in [*ring.values(), *deltas]:
         copy.wait_send()
     for i in range(ENS):
         for copy in halo_copies(i):
@@ -471,8 +479,8 @@
         *[pltpu.VMEM((D // 2, w), BF) for w in widths],
         *[pltpu.VMEM((CHIPS, ROWS, w), BF) for w in widths],
         pltpu.VMEM((ENS, ROWS, 3 * C + 2 * VP), BF),
-        dma((8,)), dma((8,)), dma((8,)), dma((ENS, 2)), dma((ENS,)), dma((ENS,)),
-        dma((ENS,)), dma((ENS,)), dma((3,)), dma((3,)), dma((3, CHIPS)), dma((3, CHIPS)),
+        dma((8,)), dma((16,)), dma((16,)), dma((ENS, 2)), dma((ENS,)), dma((ENS,)),
+        dma((12,)), dma((12,)), dma((3,)), dma((3,)), dma((3, CHIPS)), dma((3, CHIPS)),
         dma((3, ENS)), dma((3, ENS)),
     ]
     rz = pl.pallas_call(

time: 68.1 us -> 61.4 us (0.902)
  Pallas kernels: 67.4 us -> 60.7 us
    pallas_call x1, Pallas kernels: 65.5 us -> 58.8 us  [local(): pl.pallas_call(main_kernel, out_shape=jax.ShapeDtypeStruct((ENS, ROWS, 3...]
where the time goes in v4:
time: 61.4 us; the launch traced here: 61.3 us
  Pallas kernels  60.7 us (99%)
  between operations  0.64 us (1%)
    pallas_call x1, Pallas kernels, local(): pl.pallas_call(main_kernel, out_shape=jax.ShapeDtypeStruct((ENS, ROWS, 3...  58.8 us
    pallas_call x1, Pallas kernels, local(): pl.pallas_call(finish_kernel, out_shape=(full, full, full, full, jax.Shap...  1.86 us

profile of v4, /device:TPU:1, one launch (start us, length us, event | category | flops | bytes accessed | tf_op | source)
XLA Modules:
  0.0 61.3 jit_solution(5087247989342953332)
XLA Ops:
  0.6 58.8 %ensemble_gradients.1.rz_ref = bf16[8,32,640]{2,1,0:T(8,128)(2,1)} custom-call(bf16[64,1024]{1,0:T(8,128)(2,1)} %bitcast.8, bf16[256,1024]{1,0:T(8,128)(2,1)} %grid_hbm.1, s32[3,256]{1,0:T(4,128)} %bitcast.10, f32[100,256]{1,0:T(8,128)} %bitcast.9, f32[1,256]{1,0:T(1,128)} %bitcast.11, f32[1,100]{1,0:T(1,128)} %bitcast.12, bf16[1024,1024]{1,0:T(8,128)(2,1)} %wq_hbm.1, ...), custom_call_target="tpu_custom_call" | custom-call | tf_op jit(solution)/shard_map/ensemble_gradients/pallas_call | solution.py:486
  59.5 1.9 %finish.1 = (f32[32,1024]{1,0:T(8,128)}, f32[32,1024]{1,0:T(8,128)}, f32[32,1024]{1,0:T(8,128)}, f32[32,1024]{1,0:T(8,128)}, f32[32,100]{1,0:T(8,128)}) custom-call(bf16[8,32,640]{2,1,0:T(8,128)(2,1)} %ensemble_gradients.1.rz_ref, bf16[100,1024]{1,0:T(8,128)(2,1)} %bitcast.7), custom_call_target="tpu_custom_call" | custom-call | tf_op jit(solution)/shard_map/finish/pallas_call | solution.py:498

commit v5 on v4

--- a/solution.py
+++ b/solution.py
@@ -70,6 +70,9 @@
 PLACE = {0: 0, -1: 1, 1: 2, -2: 3, 2: 4, -3: 5, 3: 6, -4: 7, 4: 7}
 
 
+FAR_FIRST = sorted(range(1, CHIPS), key=lambda t: -min(t // CX, CY - t // CX) - min(t % CX, CX - t % CX))
+
+
 def main_kernel(
     x_hbm, grid_hbm, edge_ref, target_hbm, area_ref, var_ref,
     wq_hbm, wk_hbm, wv_hbm, wo_hbm, wh_hbm,
@@ -77,7 +80,7 @@
     grid_ref, target_ref, wh_ref, wq, wk, wv, wo, wht, lat, lat_t, grid_t, mix_t, q, keys, values, attended, hidden,
     delta, wkvc, kg, vg, att_all, att_low, gl, ga, s_v, s_k, oh, oh_t, q3, gq, uct, common, areaw,
     part_ab, part_v, part_qk, sib_ab, sib_v, sib_qk, sum_ab, sum_v, sum_qk, r_ab, r_v, r_qk, rz,
-    wsem, ring_s, ring_r, halo_s, halo_l, halo_r, d_s, d_r, sib_s, sib_r, xy_s, xy_r, z_s, z_r,
+    wsem, ring_s, ring_r, halo_s, halo_l, halo_r, d_s, d_r, sib_s, sib_r, xy_s, xy_r, z_s, z_r, tokens,
 ):
     e = lax.axis_index("ens")
     s = lax.axis_index("space")
@@ -101,16 +104,18 @@
     def greet(peer):
         pl.semaphore_signal(barrier, inc=1, device_id=peer, device_id_type=MESH)
 
-    greet(space_peer(1))
-    greet(space_peer(-1))
-
-    @pl.loop(1, ENS)
-    def _(d):
-        greet(ens_peer(d))
-
-    @pl.loop(1, CHIPS)
-    def _(t):
-        greet((e, chip_peer(t) * 2 + core))
+    along_x = [(e, chip_peer(1) * 2 + core), (e, chip_peer(CX - 1) * 2 + core)]
+    along_y = [(e, chip_peer(CX) * 2 + core), (e, chip_peer((CY - 1) * CX) * 2 + core)]
+    neighbours = [space_peer(1), space_peer(-1), ens_peer(1), ens_peer(-1), *along_x, *along_y]
+    for peer in neighbours:
+        greet(peer)
+
+    def give_token(i):
+        for peer in along_x if i == 0 else along_y:
+            pl.semaphore_signal(tokens.at[i], inc=1, device_id=peer, device_id_type=MESH)
+
+    def take_token(i):
+        pl.semaphore_wait(tokens.at[i], 2)
 
     def own_rows(i):
         return pl.ds(i * N + M, M)
@@ -178,11 +183,12 @@
         q[:, cols] = dot(grid_ref[...], wq[:, cols]).astype(BF)
 
     load_x.wait()
-    pl.semaphore_wait(barrier, 2 + ENS - 1 + CHIPS - 1)
+    pl.semaphore_wait(barrier, len(neighbours))
     start_halo(0)
     for half in (0, 1):
         ring[1, 1, half].start()
         ring[1, -1, half].start()
+    give_token(0)
 
     for copy in loads:
         copy.wait()
@@ -206,6 +212,8 @@
 
     wait_halo(0)
     pass_on(1, 0)
+    take_token(0)
+    give_token(1)
     for n in range(D // W):
         cols = slice(n * W, (n + 1) * W)
         keys[:, cols] = dot(lat[:N, :], wk[:, cols]).astype(BF)
@@ -227,6 +235,8 @@
         attended[:, cols] = total.astype(BF)
         if n == 1:
             pass_on(2, 0)
+            take_token(1)
+            give_token(2)
 
     pass_on(2, 1)
     start_halo(PLACE[-2])
@@ -299,6 +309,7 @@
 
     for copy in [*near1.values(), *far3.values(), *far4.values()]:
         copy.wait_recv()
+    take_token(2)
 
     fair_eps = (1.0 - FAIR_ALPHA) / ENS
     pair_coef = (1.0 - fair_eps) / (ENS * (ENS - 1))
@@ -338,8 +349,7 @@
         sibling_copy(i, part, sib).wait_recv()
         summed[...] = (part[core].astype(F32) + sib[...].astype(F32)).astype(BF)
 
-        @pl.loop(1, CHIPS)
-        def _(t):
+        for t in FAR_FIRST:
             chip_copy(i, summed, r, t).start()
 
         r[0] = summed[pl.ds(pl.multiple_of((s // 2) * ROWS, ROWS), ROWS), :]
@@ -376,22 +386,14 @@
     sibling_copy(*ab).start()
 
     for p in range(PAIRS):
-        rows = slice(p * 2 * G, (p + 1) * 2 * G)
-        both = dot(gl[rows, :], uct[...]).astype(BF)
-        both = side(both[:G], both[G:])
-        ga[p] = both
-        sums = dot(oh_t[...], att_low[p] * three(both)).astype(BF)
-        s_v[2 * p * N : (2 * p + 1) * N, :] = sums[:, :C]
-        s_v[(2 * p + 1) * N : (2 * p + 2) * N, :] = sums[:, C:]
-
-    for i in range(D // W):
-        put(part_v, i, slice(0, C), dot(lat_t[i * W : (i + 1) * W, :], s_v[...]))
-    sibling_copy(*v).start()
-    spread(*ab, sum_ab, r_ab)
-
-    gq[...] = jnp.zeros_like(gq)
+        both = dot(gl[p * 2 * G : (p + 1) * 2 * G, :], uct[...]).astype(BF)
+        ga[p] = side(both[:G], both[G:])
+
+    def to_nodes(p, sums, s_ref):
+        s_ref[2 * p * N : (2 * p + 1) * N, :] = sums[:, :C]
+        s_ref[(2 * p + 1) * N : (2 * p + 2) * N, :] = sums[:, C:]
+
     ones = same_head(W, 1.0)
-
     for p in range(PAIRS):
         gw = dot(vg[p] * three(ga[p]), ones)
         att = att_all[p]
@@ -399,22 +401,28 @@
         gs = (att * (gw - three(t[:G] + t[G : 2 * G] + t[2 * G :])) * HD**-0.5).astype(BF)
         gqe = gs.astype(F32) * kg[p].astype(F32)
         gqe = gqe[:G] + gqe[G : 2 * G] + gqe[2 * G :]
-        gq[...] += gqe[:, :C] + gqe[:, C:]
-        sums = dot(oh_t[...], gs * q3[...]).astype(BF)
-        s_k[2 * p * N : (2 * p + 1) * N, :] = sums[:, :C]
-        s_k[(2 * p + 1) * N : (2 * p + 2) * N, :] = sums[:, C:]
-
-    spread(*v, sum_v, r_v)
+        gqe = gqe[:, :C] + gqe[:, C:]
+        gq[...] = gqe if p == 0 else gq[...] + gqe
+        to_nodes(p, dot(oh_t[...], gs * q3[...]).astype(BF), s_k)
+        if p == 1:
+            spread(*ab, sum_ab, r_ab)
+
     for i in range(D // W):
         rows = slice(i * W, (i + 1) * W)
         put(part_qk, i, slice(0, C), dot(grid_t[rows, :], gq[...].astype(BF)))
         put(part_qk, i, slice(C, 2 * C), dot(lat_t[rows, :], s_k[...]))
     sibling_copy(*qk).start()
+    for p in range(PAIRS):
+        to_nodes(p, dot(oh_t[...], att_low[p] * three(ga[p])).astype(BF), s_v)
+    spread(*qk, sum_qk, r_qk)
+    for i in range(D // W):
+        put(part_v, i, slice(0, C), dot(lat_t[i * W : (i + 1) * W, :], s_v[...]))
+    sibling_copy(*v).start()
     qk_cols, v_cols, ab_cols = slice(0, 2 * C), slice(2 * C, 3 * C), slice(3 * C, 3 * C + 2 * VP)
-    spread(*qk, sum_qk, r_qk)
     collect(0, sum_ab, r_ab, ab_cols)
+    spread(*v, sum_v, r_v)
+    collect(2, sum_qk, r_qk, qk_cols)
     collect(1, sum_v, r_v, v_cols)
-    collect(2, sum_qk, r_qk, qk_cols)
 
     for copy in [*ring.values(), *deltas]:
         copy.wait_send()
@@ -422,7 +430,7 @@
         for copy in halo_copies(i):
             copy.wait_send()
     stores = []
-    for i, summed, r, cols in ((0, sum_ab, r_ab, ab_cols), (1, sum_v, r_v, v_cols), (2, sum_qk, r_qk, qk_cols)):
+    for i, summed, r, cols in ((0, sum_ab, r_ab, ab_cols), (2, sum_qk, r_qk, qk_cols), (1, sum_v, r_v, v_cols)):
         sibling_copy(*(ab, v, qk)[i]).wait_send()
 
         @pl.loop(1, CHIPS)
@@ -481,7 +489,7 @@
         pltpu.VMEM((ENS, ROWS, 3 * C + 2 * VP), BF),
         dma((8,)), dma((16,)), dma((16,)), dma((ENS, 2)), dma((ENS,)), dma((ENS,)),
         dma((12,)), dma((12,)), dma((3,)), dma((3,)), dma((3, CHIPS)), dma((3, CHIPS)),
-        dma((3, ENS)), dma((3, ENS)),
+        dma((3, ENS)), dma((3, ENS)), pltpu.SemaphoreType.REGULAR((3,)),
     ]
     rz = pl.pallas_call(
         main_kernel,

time: 61.4 us -> 59.9 us (0.976)
  Pallas kernels: 60.7 us -> 59 us
    pallas_call x1, Pallas kernels: 58.8 us -> 57.1 us  [local(): pl.pallas_call(main_kernel, out_shape=jax.ShapeDtypeStruct((ENS, ROWS, 3...]
where the time goes in v5:
time: 59.9 us; the launch traced here: 59.6 us
  Pallas kernels  59 us (98%)
  between operations  0.64 us (1%)
    pallas_call x1, Pallas kernels, local(): pl.pallas_call(main_kernel, out_shape=jax.ShapeDtypeStruct((ENS, ROWS, 3...  57.1 us
    pallas_call x1, Pallas kernels, local(): pl.pallas_call(finish_kernel, out_shape=(full, full, full, full, jax.Shap...  1.86 us

profile of v5, /device:TPU:1, one launch (start us, length us, event | category | flops | bytes accessed | tf_op | source)
XLA Modules:
  0.0 59.6 jit_solution(6161011851366926651)
XLA Ops:
  0.6 57.1 %ensemble_gradients.1.rz_ref = bf16[8,32,640]{2,1,0:T(8,128)(2,1)} custom-call(bf16[64,1024]{1,0:T(8,128)(2,1)} %bitcast.8, bf16[256,1024]{1,0:T(8,128)(2,1)} %grid_hbm.1, s32[3,256]{1,0:T(4,128)} %bitcast.10, f32[100,256]{1,0:T(8,128)} %bitcast.9, f32[1,256]{1,0:T(1,128)} %bitcast.11, f32[1,100]{1,0:T(1,128)} %bitcast.12, bf16[1024,1024]{1,0:T(8,128)(2,1)} %wq_hbm.1, ...), custom_call_target="tpu_custom_call" | custom-call | tf_op jit(solution)/shard_map/ensemble_gradients/pallas_call | solution.py:494
  57.7 1.9 %finish.1 = (f32[32,1024]{1,0:T(8,128)}, f32[32,1024]{1,0:T(8,128)}, f32[32,1024]{1,0:T(8,128)}, f32[32,1024]{1,0:T(8,128)}, f32[32,100]{1,0:T(8,128)}) custom-call(bf16[8,32,640]{2,1,0:T(8,128)(2,1)} %ensemble_gradients.1.rz_ref, bf16[100,1024]{1,0:T(8,128)(2,1)} %bitcast.7), custom_call_target="tpu_custom_call" | custom-call | tf_op jit(solution)/shard_map/finish/pallas_call | solution.py:506

commit v6 on v5

--- a/solution.py
+++ b/solution.py
@@ -176,12 +176,6 @@
         for copy in halo_copies(i):
             copy.wait_recv()
 
-    load_grid.wait()
-    load_wq.wait()
-    for n in range(D // W):
-        cols = slice(n * W, (n + 1) * W)
-        q[:, cols] = dot(grid_ref[...], wq[:, cols]).astype(BF)
-
     load_x.wait()
     pl.semaphore_wait(barrier, len(neighbours))
     start_halo(0)
@@ -189,6 +183,12 @@
         ring[1, 1, half].start()
         ring[1, -1, half].start()
     give_token(0)
+
+    load_grid.wait()
+    load_wq.wait()
+    for n in range(D // W):
+        cols = slice(n * W, (n + 1) * W)
+        q[:, cols] = dot(grid_ref[...], wq[:, cols]).astype(BF)
 
     for copy in loads:
         copy.wait()
@@ -200,14 +200,10 @@
     for j in range(KNN):
         oh_t[:, j * G : (j + 1) * G] = jnp.where(slot_rows[j : j + 1, :] == node, 1.0, 0.0).astype(BF)
     oh[...] = oh_t[...].T
-    grid_t[...] = grid_ref[...].T
-    var_row = jnp.concatenate([var_ref[...], jnp.zeros((1, VP - VAR), F32)], axis=1)
-    areaw[...] = jnp.broadcast_to(area_ref[...], (VP, G)).T * var_row
     common[...] = dot_nt(grid_ref[...], wht[...])
     hs = pl.ds(pl.multiple_of(e * C, C), C)
     wkvc[:, :C] = wk[:, hs]
     wkvc[:, C:] = wv[:, hs]
-    uct[...] = dot_nt(wht[...], wo[hs, :]).astype(BF)
     q3[...] = three(side(q[:, hs], q[:, hs]))
 
     wait_halo(0)
@@ -282,6 +278,9 @@
             att_low[p, j * G : (j + 1) * G, :] = att[j].astype(BF)
         lat_t[:, rows] = lat[rows, :].T
 
+    var_row = jnp.concatenate([var_ref[...], jnp.zeros((1, VP - VAR), F32)], axis=1)
+    areaw[...] = jnp.broadcast_to(area_ref[...], (VP, G)).T * var_row
+    uct[...] = dot_nt(wht[...], wo[hs, :]).astype(BF)
     padded = jnp.concatenate([target_ref[...], jnp.zeros((VP - VAR, G), F32)], axis=0)
     common[...] = common[...] - padded.T
     mix_t[:D, :] = attended[...].T
@@ -292,6 +291,7 @@
     start_halo(PLACE[-3])
     start_halo(PLACE[3])
     mix_t[D:, :] = hidden[...].T
+    grid_t[...] = grid_ref[...].T
     pass_delta_on(0)
     wait_halo(2)
     wait_halo(3)
@@ -303,20 +303,11 @@
     wait_halo(4)
     wait_halo(5)
     prepare(2)
-    wait_halo(6)
-    wait_halo(7)
-    prepare(3)
-
-    for copy in [*near1.values(), *far3.values(), *far4.values()]:
-        copy.wait_recv()
-    take_token(2)
-
     fair_eps = (1.0 - FAIR_ALPHA) / ENS
     pair_coef = (1.0 - fair_eps) / (ENS * (ENS - 1))
     step_rows = 16
 
-    @pl.loop(0, G // step_rows)
-    def _(i):
+    def loss_gradient(i):
         rows = pl.ds(pl.multiple_of(i * step_rows, step_rows), step_rows)
         dev = [delta[m, rows, :].astype(F32) for m in range(ENS)]
         pair = [None] * ENS
@@ -330,6 +321,23 @@
         for m in range(ENS):
             grad = scale * (slope(dev[m] + shift) * (1.0 / ENS) - pair_coef * pair[m])
             gl[pl.ds(pl.multiple_of(m * G + i * step_rows, step_rows), step_rows), :] = grad.astype(BF)
+
+    def loss_gradient_of(half):
+        if half == 0:
+            near1[1].wait_recv()
+            near1[-1].wait_recv()
+        far4[1 - 2 * half].wait_recv()
+        far3[1, half].wait_recv()
+        far3[-1, half].wait_recv()
+        steps = G // step_rows // 2
+        pl.loop(half * steps, (half + 1) * steps)(loss_gradient)
+
+    loss_gradient_of(0)
+    wait_halo(6)
+    wait_halo(7)
+    prepare(3)
+    loss_gradient_of(1)
+    take_token(2)
 
     def sibling_copy(i, part, sib):
         return pltpu.make_async_remote_copy(

time: 59.9 us -> 59.3 us (0.990); the launches traced: 59.6 us -> 58.2 us
  Pallas kernels: 59 us -> 57.6 us
    pallas_call x1, Pallas kernels: 57.1 us -> 55.7 us  [local(): pl.pallas_call(main_kernel, out_shape=jax.ShapeDtypeStruct((ENS, ROWS, 3...]
where the time goes in v6:
time: 59.3 us; the launch traced here: 58.2 us
  Pallas kernels  57.6 us (97%)
  between operations  0.64 us (1%)
    pallas_call x1, Pallas kernels, local(): pl.pallas_call(main_kernel, out_shape=jax.ShapeDtypeStruct((ENS, ROWS, 3...  55.7 us
    pallas_call x1, Pallas kernels, local(): pl.pallas_call(finish_kernel, out_shape=(full, full, full, full, jax.Shap...  1.86 us

profile of v6, /device:TPU:1, one launch (start us, length us, event | category | flops | bytes accessed | tf_op | source)
XLA Modules:
  0.0 58.2 jit_solution(15897563650667313898)
XLA Ops:
  0.6 55.7 %ensemble_gradients.1.rz_ref = bf16[8,32,640]{2,1,0:T(8,128)(2,1)} custom-call(bf16[64,1024]{1,0:T(8,128)(2,1)} %bitcast.8, bf16[256,1024]{1,0:T(8,128)(2,1)} %grid_hbm.1, s32[3,256]{1,0:T(4,128)} %bitcast.10, f32[100,256]{1,0:T(8,128)} %bitcast.9, f32[1,256]{1,0:T(1,128)} %bitcast.11, f32[1,100]{1,0:T(1,128)} %bitcast.12, bf16[1024,1024]{1,0:T(8,128)(2,1)} %wq_hbm.1, ...), custom_call_target="tpu_custom_call" | custom-call | tf_op jit(solution)/shard_map/ensemble_gradients/pallas_call | solution.py:502
  56.4 1.9 %finish.1 = (f32[32,1024]{1,0:T(8,128)}, f32[32,1024]{1,0:T(8,128)}, f32[32,1024]{1,0:T(8,128)}, f32[32,1024]{1,0:T(8,128)}, f32[32,100]{1,0:T(8,128)}) custom-call(bf16[8,32,640]{2,1,0:T(8,128)(2,1)} %ensemble_gradients.1.rz_ref, bf16[100,1024]{1,0:T(8,128)(2,1)} %bitcast.7), custom_call_target="tpu_custom_call" | custom-call | tf_op jit(solution)/shard_map/finish/pallas_call | solution.py:514

commit v7 on v6

--- a/solution.py
+++ b/solution.py
@@ -427,8 +427,8 @@
         put(part_v, i, slice(0, C), dot(lat_t[i * W : (i + 1) * W, :], s_v[...]))
     sibling_copy(*v).start()
     qk_cols, v_cols, ab_cols = slice(0, 2 * C), slice(2 * C, 3 * C), slice(3 * C, 3 * C + 2 * VP)
+    spread(*v, sum_v, r_v)
     collect(0, sum_ab, r_ab, ab_cols)
-    spread(*v, sum_v, r_v)
     collect(2, sum_qk, r_qk, qk_cols)
     collect(1, sum_v, r_v, v_cols)
 

time: 59.3 us -> 60.2 us (1.015); the launches traced: 58.2 us -> 60 us
  Pallas kernels: 57.6 us -> 59.4 us
    pallas_call x1, Pallas kernels: 55.7 us -> 57.5 us  [local(): pl.pallas_call(main_kernel, out_shape=jax.ShapeDtypeStruct((ENS, ROWS, 3...]
where the time goes in v7:
time: 60.2 us; the launch traced here: 60 us
  Pallas kernels  59.4 us (99%)
  between operations  0.64 us (1%)
    pallas_call x1, Pallas kernels, local(): pl.pallas_call(main_kernel, out_shape=jax.ShapeDtypeStruct((ENS, ROWS, 3...  57.5 us
    pallas_call x1, Pallas kernels, local(): pl.pallas_call(finish_kernel, out_shape=(full, full, full, full, jax.Shap...  1.86 us

profile of v7, /device:TPU:1, one launch (start us, length us, event | category | flops | bytes accessed | tf_op | source)
XLA Modules:
  0.0 60.0 jit_solution(9508810794105207224)
XLA Ops:
  0.6 57.5 %ensemble_gradients.1.rz_ref = bf16[8,32,640]{2,1,0:T(8,128)(2,1)} custom-call(bf16[64,1024]{1,0:T(8,128)(2,1)} %bitcast.8, bf16[256,1024]{1,0:T(8,128)(2,1)} %grid_hbm.1, s32[3,256]{1,0:T(4,128)} %bitcast.10, f32[100,256]{1,0:T(8,128)} %bitcast.9, f32[1,256]{1,0:T(1,128)} %bitcast.11, f32[1,100]{1,0:T(1,128)} %bitcast.12, bf16[1024,1024]{1,0:T(8,128)(2,1)} %wq_hbm.1, ...), custom_call_target="tpu_custom_call" | custom-call | tf_op jit(solution)/shard_map/ensemble_gradients/pallas_call | solution.py:502
  58.2 1.9 %finish.1 = (f32[32,1024]{1,0:T(8,128)}, f32[32,1024]{1,0:T(8,128)}, f32[32,1024]{1,0:T(8,128)}, f32[32,1024]{1,0:T(8,128)}, f32[32,100]{1,0:T(8,128)}) custom-call(bf16[8,32,640]{2,1,0:T(8,128)(2,1)} %ensemble_gradients.1.rz_ref, bf16[100,1024]{1,0:T(8,128)(2,1)} %bitcast.7), custom_call_target="tpu_custom_call" | custom-call | tf_op jit(solution)/shard_map/finish/pallas_call | solution.py:514
